TPU v7x, 32 devices: a whole 2x2x4 slice. The times are simulated.
32 devices in a mesh: dp: 16 (over z, x, core), tensor: 2 (over y).
Axes of the slice: x: 2, y: 2, z: 4, core: 2. Of those that a mesh axis runs over, the one named last changes fastest.
Arguments:
- tokens: bfloat16 [16384, 1024], P(('dp', 'tensor')), may hold values from -6 to 6
- slot_seq: int32 [16384], P('dp'), may hold values from 0 to 7, as said below
- seq_len: int32 [128], P('dp'), may hold values from 0 to 1024, as said below
- ln1_gain: bfloat16 [1024], P('dp'), may hold values from 0.5 to 1.5
- ln1_shift: bfloat16 [1024], P('dp'), may hold values from -3 to 3
- qkv_weight: bfloat16 [1024, 3, 1024], P('dp', None, 'tensor'), may hold values from -0.1875 to 0.1875
- qkv_bias: bfloat16 [2, 16, 64], P(None, 'tensor', 'dp'), may hold values from -3 to 3
- out_weight: bfloat16 [1024, 1024], P('tensor', 'dp'), may hold values from -0.75 to 0.75
- out_bias: bfloat16 [1024], P('dp'), may hold values from -3 to 3
- ln2_gain: bfloat16 [1024], P('dp'), may hold values from 0.5 to 1.5
- ln2_shift: bfloat16 [1024], P('dp'), may hold values from -3 to 3
- up_weight: bfloat16 [1024, 4096], P('dp', 'tensor'), may hold values from -0.1875 to 0.1875
- up_bias: bfloat16 [64, 64], P('tensor', 'dp'), may hold values from -3 to 3
- down_weight: bfloat16 [4096, 1024], P('tensor', 'dp'), may hold values from -0.09375 to 0.09375
- down_bias: bfloat16 [1024], P('dp'), may hold values from -3 to 3
- cotangent: bfloat16 [16384, 1024], P(('dp', 'tensor')), may hold values from -6 to 6
Outputs:
- output: float32 [16384, 1024], P(('dp', 'tensor'))
- grad_tokens: float32 [16384, 1024], P(('dp', 'tensor'))
- grad_ln1_gain: float32 [1024], P('dp')
- grad_ln1_shift: float32 [1024], P('dp')
- grad_qkv_weight: float32 [1024, 3, 1024], P('dp', None, 'tensor')
- grad_qkv_bias: float32 [2, 16, 64], P(None, 'tensor', 'dp')
- grad_out_weight: float32 [1024, 1024], P('tensor', 'dp')
- grad_out_bias: float32 [1024], P('dp')
- grad_ln2_gain: float32 [1024], P('dp')
- grad_ln2_shift: float32 [1024], P('dp')
- grad_up_weight: float32 [1024, 4096], P('dp', 'tensor')
- grad_up_bias: float32 [64, 64], P('tensor', 'dp')
- grad_down_weight: float32 [4096, 1024], P('tensor', 'dp')
- grad_down_bias: float32 [1024], P('dp')
Inputs may be any that keep to these rules, and one draw needn't show every extreme that they name: Within each group of 1024 slots, slot_seq starts at 0, never falls, rises by one at a time and changes only at multiples of 128; a sequence's live tokens are its first slots; some group holds 8 sequences of one block each. `seq_len`: A length is 0 exactly for sequence numbers that mark empty blocks or are unused; a live sequence fits its blocks and has at least one live token; some group holds one sequence of 1024 live tokens.
All inputs are finite; a program needn't handle non-finite values.
Results may differ from a plain program's by a relative error of at most 0.02.
Values may be sent and summed in bfloat16 or wider, within the bound.
A program may use at most 192 MiB of HBM per device.

v0:
```python
import jax
import jax.numpy as jnp
from jax import lax
from jax.sharding import PartitionSpec as P

HD = 64


epsilon = 1e-05
masked_fill = -1e30
gelu_root = 0.7978845608028654
gelu_cubic = 0.044715


def layer_norm(hidden, gain, shift):
    center = hidden - jnp.mean(hidden, axis=-1, keepdims=True)
    inverse = lax.rsqrt(jnp.mean(center * center, axis=-1, keepdims=True) + epsilon)
    normed = center * inverse
    return (normed * gain + shift, normed, inverse)


def norm_back(upstream, gain, normed, inverse):
    scaled = upstream * gain
    return inverse * (
        scaled
        - jnp.mean(scaled, axis=-1, keepdims=True)
        - normed * jnp.mean(scaled * normed, axis=-1, keepdims=True)
    )


def gelu_value(inputs):
    tangent = jnp.tanh(gelu_root * (inputs + gelu_cubic * inputs * inputs * inputs))
    return 0.5 * inputs * (1.0 + tangent)


def gelu_slope(inputs):
    tangent = jnp.tanh(gelu_root * (inputs + gelu_cubic * inputs * inputs * inputs))
    return 0.5 * (1.0 + tangent) + 0.5 * inputs * (1.0 - tangent * tangent) * gelu_root * (
        1.0 + 3.0 * gelu_cubic * inputs * inputs
    )


def live_slots(slot_seq, seq_len):
    numbers = seq_len.shape[0]
    onehot = (slot_seq[:, None] == jnp.arange(numbers, dtype=jnp.int32)[None, :]).astype(jnp.int32)
    counts = jnp.sum(onehot, axis=0, dtype=jnp.int32)
    first_slot = jnp.cumsum(counts, dtype=jnp.int32) - counts
    run_start = jnp.sum(onehot * first_slot[None, :], axis=1, dtype=jnp.int32)
    run_length = jnp.sum(onehot * seq_len[None, :], axis=1, dtype=jnp.int32)
    places = jnp.arange(slot_seq.shape[0], dtype=jnp.int32) - run_start
    return places < run_length


def allowed_rows(slot_seq, live, first_row, row_count):
    seq_query = slot_seq[first_row : first_row + row_count]
    query_index = first_row + jnp.arange(row_count, dtype=jnp.int32)
    key_index = jnp.arange(slot_seq.shape[0], dtype=jnp.int32)
    return (
        (seq_query[:, None] == slot_seq[None, :])
        & (key_index[None, :] <= query_index[:, None])
        & live[None, :]
    )


def block_scores(queries, key_rows, allowed):
    scores = jnp.einsum(
        "qhd,khd->hqk", queries, key_rows, preferred_element_type=jnp.float32
    ) * queries.shape[-1] ** (-0.5)
    return jnp.where(allowed[None], scores, masked_fill)


def local(
    tokens,
    slot_seq,
    seq_len,
    ln1_gain,
    ln1_shift,
    qkv_weight,
    qkv_bias,
    out_weight,
    out_bias,
    ln2_gain,
    ln2_shift,
    up_weight,
    up_bias,
    down_weight,
    down_bias,
    cotangent,
):
    f32 = jnp.float32
    bf16 = jnp.bfloat16
    own_rows = tokens.shape[0]
    slots = slot_seq.shape[0]
    (
        gain_one,
        shift_one,
        w_qkv,
        w_up,
        bias_out,
        gain_two,
        shift_two,
        bias_down,
        w_out,
        w_down,
        bias_up,
        bias_qkv,
    ) = (
        lax.all_gather(ln1_gain, "dp", axis=0, tiled=True),
        lax.all_gather(ln1_shift, "dp", axis=0, tiled=True),
        lax.all_gather(qkv_weight, "dp", axis=0, tiled=True),
        lax.all_gather(up_weight, "dp", axis=0, tiled=True),
        lax.all_gather(out_bias, "dp", axis=0, tiled=True),
        lax.all_gather(ln2_gain, "dp", axis=0, tiled=True),
        lax.all_gather(ln2_shift, "dp", axis=0, tiled=True),
        lax.all_gather(down_bias, "dp", axis=0, tiled=True),
        lax.all_gather(out_weight, "dp", axis=1, tiled=True),
        lax.all_gather(down_weight, "dp", axis=1, tiled=True),
        lax.all_gather(up_bias, "dp", axis=1, tiled=True),
        lax.all_gather(qkv_bias, "dp", axis=2, tiled=True),
    )
    heads_here = w_qkv.shape[2] // HD
    live = live_slots(slot_seq, seq_len)
    own_live = lax.dynamic_slice_in_dim(live, lax.axis_index("tensor") * own_rows, own_rows)
    inputs = tokens.astype(f32)
    a1_full, normed_one, inverse_one = layer_norm(
        inputs, gain_one.astype(f32), shift_one.astype(f32)
    )
    a1_all = lax.all_gather(a1_full.astype(bf16), "tensor", axis=0, tiled=True)
    qkv_full = jnp.einsum("td,dck->tck", a1_all, w_qkv, preferred_element_type=f32)
    bias_rows = bias_qkv.reshape(2, heads_here * HD).astype(f32)
    bias_all = jnp.stack([bias_rows[0], jnp.zeros_like(bias_rows[0]), bias_rows[1]], axis=0)
    qkv = (qkv_full + bias_all[None]).astype(bf16)
    queries = qkv[:, 0].reshape(slots, heads_here, HD)
    key_rows = qkv[:, 1].reshape(slots, heads_here, HD)
    values = qkv[:, 2].reshape(slots, heads_here, HD)
    rows_query = min(512, slots)
    head_blocks = []
    lse_blocks = []
    for first_row in range(0, slots, rows_query):
        allowed = allowed_rows(slot_seq, live, first_row, rows_query)
        scores = block_scores(queries[first_row : first_row + rows_query], key_rows, allowed)
        top = jnp.max(scores, axis=-1, keepdims=True)
        log_total = top + jnp.log(jnp.sum(jnp.exp(scores - top), axis=-1, keepdims=True))
        probs = jnp.exp(scores - log_total).astype(bf16)
        head_blocks.append(
            jnp.einsum("hqk,khd->qhd", probs, values, preferred_element_type=f32).astype(bf16)
        )
        lse_blocks.append(log_total)
    heads = jnp.concatenate(head_blocks, axis=0)
    heads_flat = heads.reshape(slots, heads_here * HD)
    piece = heads_flat
    attn = lax.psum_scatter(
        jnp.dot(piece, w_out, preferred_element_type=f32)
        .astype(bf16)
        .astype(f32)
        .astype(jnp.bfloat16),
        "tensor",
        scatter_dimension=0,
        tiled=True,
    ).astype(jnp.float32)
    hidden_one = inputs + attn + bias_out.astype(f32)
    a2_full, normed_two, inverse_two = layer_norm(
        hidden_one, gain_two.astype(f32), shift_two.astype(f32)
    )
    a2_all = lax.all_gather(a2_full.astype(bf16), "tensor", axis=0, tiled=True)
    pre = jnp.dot(a2_all, w_up, preferred_element_type=f32) + bias_up.reshape(-1).astype(f32)
    act = gelu_value(pre).astype(bf16)
    piece = act
    mlp = lax.psum_scatter(
        jnp.dot(piece, w_down, preferred_element_type=f32)
        .astype(bf16)
        .astype(f32)
        .astype(jnp.bfloat16),
        "tensor",
        scatter_dimension=0,
        tiled=True,
    ).astype(jnp.float32)
    output = jnp.where(own_live[:, None], hidden_one + mlp + bias_down.astype(f32), 0.0)
    gain_one, gain_two, w_qkv, w_up, w_out, w_down = (
        lax.all_gather(ln1_gain, "dp", axis=0, tiled=True),
        lax.all_gather(ln2_gain, "dp", axis=0, tiled=True),
        lax.all_gather(qkv_weight, "dp", axis=0, tiled=True),
        lax.all_gather(up_weight, "dp", axis=0, tiled=True),
        lax.all_gather(out_weight, "dp", axis=1, tiled=True),
        lax.all_gather(down_weight, "dp", axis=1, tiled=True),
    )
    grad_h2 = jnp.where(own_live[:, None], cotangent.astype(f32), 0.0)
    grad_down_bias = jnp.sum(grad_h2, axis=0)
    grad_h2_all = lax.all_gather(grad_h2.astype(bf16), "tensor", axis=0, tiled=True)
    grad_down_weight = jnp.einsum("tf,td->fd", act, grad_h2_all, preferred_element_type=f32)
    grad_pre = jnp.einsum(
        "td,fd->tf", grad_h2_all, w_down, preferred_element_type=f32
    ) * gelu_slope(pre)
    grad_up_bias = jnp.sum(grad_pre, axis=0).reshape(-1, HD)
    grad_pre_b = grad_pre.astype(bf16)
    grad_up_weight = jnp.einsum("td,tf->df", a2_all, grad_pre_b, preferred_element_type=f32)
    piece = grad_pre_b
    grad_a2 = lax.psum_scatter(
        jnp.einsum("tf,df->td", piece, w_up, preferred_element_type=f32)
        .astype(bf16)
        .astype(f32)
        .astype(jnp.bfloat16),
        "tensor",
        scatter_dimension=0,
        tiled=True,
    ).astype(jnp.float32)
    grad_ln2_gain = jnp.sum(grad_a2 * normed_two, axis=0)
    grad_ln2_shift = jnp.sum(grad_a2, axis=0)
    grad_h1 = grad_h2 + norm_back(grad_a2, gain_two.astype(f32), normed_two, inverse_two)
    grad_out_bias = jnp.sum(grad_h1, axis=0)
    grad_h1_all = lax.all_gather(grad_h1.astype(bf16), "tensor", axis=0, tiled=True)
    grad_out_weight = jnp.einsum("tk,td->kd", heads_flat, grad_h1_all, preferred_element_type=f32)
    grad_heads = (
        jnp.einsum("td,kd->tk", grad_h1_all, w_out, preferred_element_type=f32)
        .astype(bf16)
        .reshape(slots, heads_here, HD)
    )
    grad_keys = jnp.zeros((slots, heads_here, HD), f32)
    grad_values = jnp.zeros((slots, heads_here, HD), f32)
    query_blocks = []
    for block_number, first_row in enumerate(range(0, slots, rows_query)):
        allowed = allowed_rows(slot_seq, live, first_row, rows_query)
        block_queries = queries[first_row : first_row + rows_query]
        scores = block_scores(block_queries, key_rows, allowed)
        probs_full = jnp.exp(scores - lse_blocks[block_number])
        probs = probs_full.astype(bf16)
        block_grad = grad_heads[first_row : first_row + rows_query]
        block_heads = heads[first_row : first_row + rows_query]
        delta = jnp.sum(block_grad.astype(f32) * block_heads.astype(f32), axis=-1).T
        grad_probs = jnp.einsum("qhd,khd->hqk", block_grad, values, preferred_element_type=f32)
        grad_scores = (probs_full * (grad_probs - delta[:, :, None]) * HD ** (-0.5)).astype(bf16)
        query_blocks.append(
            jnp.einsum("hqk,khd->qhd", grad_scores, key_rows, preferred_element_type=f32)
        )
        grad_keys = grad_keys + jnp.einsum(
            "hqk,qhd->khd", grad_scores, block_queries, preferred_element_type=f32
        )
        grad_values = grad_values + jnp.einsum(
            "hqk,qhd->khd", probs, block_grad, preferred_element_type=f32
        )
    grad_queries = jnp.concatenate(query_blocks, axis=0)
    grad_qkv_full = jnp.stack([grad_queries, grad_keys, grad_values], axis=1).reshape(
        slots, 3, heads_here * HD
    )
    grad_qkv_bias = jnp.stack([jnp.sum(grad_queries, axis=0), jnp.sum(grad_values, axis=0)], axis=0)
    grad_qkv = grad_qkv_full.astype(bf16)
    grad_qkv_weight = jnp.einsum("td,tck->dck", a1_all, grad_qkv, preferred_element_type=f32)
    piece = grad_qkv
    grad_a1 = lax.psum_scatter(
        jnp.einsum("tck,dck->td", piece, w_qkv, preferred_element_type=f32)
        .astype(bf16)
        .astype(f32)
        .astype(jnp.bfloat16),
        "tensor",
        scatter_dimension=0,
        tiled=True,
    ).astype(jnp.float32)
    grad_ln1_gain = jnp.sum(grad_a1 * normed_one, axis=0)
    grad_ln1_shift = jnp.sum(grad_a1, axis=0)
    grad_tokens = grad_h1 + norm_back(grad_a1, gain_one.astype(f32), normed_one, inverse_one)
    (
        sum_qkv_w,
        sum_up_w,
        sum_out_b,
        sum_gain_one,
        sum_shift_one,
        sum_gain_two,
        sum_shift_two,
        sum_down_b,
        sum_out_w,
        sum_down_w,
        sum_up_b,
        sum_qkv_b,
    ) = (
        lax.psum_scatter(
            grad_qkv_weight.astype(jnp.bfloat16), "dp", scatter_dimension=0, tiled=True
        ).astype(jnp.float32),
        lax.psum_scatter(
            grad_up_weight.astype(jnp.bfloat16), "dp", scatter_dimension=0, tiled=True
        ).astype(jnp.float32),
        lax.psum_scatter(
            grad_out_bias.astype(jnp.bfloat16), "dp", scatter_dimension=0, tiled=True
        ).astype(jnp.float32),
        lax.psum_scatter(
            grad_ln1_gain.astype(jnp.bfloat16), "dp", scatter_dimension=0, tiled=True
        ).astype(jnp.float32),
        lax.psum_scatter(
            grad_ln1_shift.astype(jnp.bfloat16), "dp", scatter_dimension=0, tiled=True
        ).astype(jnp.float32),
        lax.psum_scatter(
            grad_ln2_gain.astype(jnp.bfloat16), "dp", scatter_dimension=0, tiled=True
        ).astype(jnp.float32),
        lax.psum_scatter(
            grad_ln2_shift.astype(jnp.bfloat16), "dp", scatter_dimension=0, tiled=True
        ).astype(jnp.float32),
        lax.psum_scatter(
            grad_down_bias.astype(jnp.bfloat16), "dp", scatter_dimension=0, tiled=True
        ).astype(jnp.float32),
        lax.psum_scatter(
            grad_out_weight.astype(jnp.bfloat16), "dp", scatter_dimension=1, tiled=True
        ).astype(jnp.float32),
        lax.psum_scatter(
            grad_down_weight.astype(jnp.bfloat16), "dp", scatter_dimension=1, tiled=True
        ).astype(jnp.float32),
        lax.psum_scatter(
            grad_up_bias.astype(jnp.bfloat16), "dp", scatter_dimension=1, tiled=True
        ).astype(jnp.float32),
        lax.psum_scatter(
            grad_qkv_bias.astype(jnp.bfloat16), "dp", scatter_dimension=2, tiled=True
        ).astype(jnp.float32),
    )
    sum_out_b, sum_gain_one, sum_shift_one, sum_gain_two, sum_shift_two, sum_down_b = lax.psum(
        (sum_out_b, sum_gain_one, sum_shift_one, sum_gain_two, sum_shift_two, sum_down_b), "tensor"
    )
    return (
        output,
        grad_tokens,
        sum_gain_one,
        sum_shift_one,
        sum_qkv_w,
        sum_qkv_b,
        sum_out_w,
        sum_out_b,
        sum_gain_two,
        sum_shift_two,
        sum_up_w,
        sum_up_b,
        sum_down_w,
        sum_down_b,
    )


def solution(mesh):
    placed = (
        P(("dp", "tensor"), None),
        P("dp"),
        P("dp"),
        P("dp"),
        P("dp"),
        P("dp", None, "tensor"),
        P(None, "tensor", "dp"),
        P("tensor", "dp"),
        P("dp"),
        P("dp"),
        P("dp"),
        P("dp", "tensor"),
        P("tensor", "dp"),
        P("tensor", "dp"),
        P("dp"),
        P(("dp", "tensor"), None),
    )
    return jax.shard_map(
        local,
        mesh=mesh,
        in_specs=placed,
        out_specs=(
            P(("dp", "tensor"), None),
            P(("dp", "tensor"), None),
            P("dp"),
            P("dp"),
            P("dp", None, "tensor"),
            P(None, "tensor", "dp"),
            P("tensor", "dp"),
            P("dp"),
            P("dp"),
            P("dp"),
            P("dp", "tensor"),
            P("tensor", "dp"),
            P("tensor", "dp"),
            P("dp"),
        ),
        check_vma=False,
    )
```

profile of v0, /device:TPU:0, one launch (start us, length us, event | category | flops | bytes accessed | tf_op | source)
XLA Modules:
  0.0 865.3 jit_solution(14744224330226859478)
XLA Ops:
  16.6 62.9 %all-reduce.16 = (bf16[1024]{0:T(1024)(128)(2,1)S(1)}, bf16[1024]{0:T(1024)(128)(2,1)S(1)}, bf16[1024]{0:T(1024)(128)(2,1)S(1)}, bf16[1024]{0:T(1024)(128)(2,1)S(1)}, bf16[1024]{0:T(1024)(128)(2,1)S(1)}) all-reduce(bf16[1024]{0:T(1024)(128)(2,1)S(1)} %dynamic-update-slice.4, ...), channel_id=1, replica_groups=mesh['dp'=16,'tensor'=2] {'dp'}, use_global_device_ids=true, to_apply=%add.4 | all-reduce | flops 5120 | bytes 20480
  84.1 17.7 %all_gather.58 = bf16[2,8,64]{1,0,2:T(2,128)(2,1)S(1)} all-gather(bf16[2,8,4]{1,0,2:T(2,128)(2,1)S(1)} %copy.52), channel_id=1, replica_groups=mesh['dp'=16,'tensor'=2] {'dp'}, dimensions={2}, use_global_device_ids=true | all-gather | bytes 2176 | tf_op jit(solution)/shard_map/all_gather | solution.py:119
  103.8 9.0 %all-gather.10.cloned.1.call-done = bf16[1024,1024]{1,0:T(8,128)(2,1)} async-done(((bf16[512,1024]{1,0:T(8,128)(2,1)}), bf16[1024,1024]{1,0:T(8,128)(2,1)}) %all-gather.10.cloned.1.call-update) | async-done | bytes 2097168 | tf_op jit(solution)/shard_map/all_gather | solution.py:128
  112.7 47.4 %all-gather.12.cloned.1.call-done = bf16[1024,3,512]{2,0,1:T(8,128)(2,1)} async-done(((bf16[64,3,512]{2,0,1:T(8,128)(2,1)}), bf16[1024,3,512]{2,0,1:T(8,128)(2,1)}) %all-gather.12.cloned.1.call-update) | async-done | bytes 3145744 | tf_op jit(solution)/shard_map/all_gather | solution.py:110
  169.5 7.8 fusion.2
  177.3 13.6 %exponential_reduce_fusion = (f32[8,512]{1,0:T(8,128)S(1)}, f32[8,512]{1,0:T(8,128)S(1)}) fusion(f32[8,512,1024]{2,1,0:T(8,128)S(1)} %get-tuple-element.110, f32[8,512]{1,0:T(8,128)S(1)} %get-tuple-element.109, pred[512,1024]{1,0:T(8,128)(4,1)S(1)} %get-tuple-element.104, f32[8,512]{1,0:T(8,128)S(1)} %get-tuple-element.111, ...), kind=kLoop, calls=%fused_computation.3 | loop fusion | flops 33546240 | bytes 34668544 | tf_op jit(solution)/shard_map/reduce_sum | solution.py:143
  190.9 8.1 fusion.48
  209.3 30.3 %reduce-scatter.11.cloned.1.call-done = bf16[512,1024]{1,0:T(8,128)(2,1)} async-done(((bf16[1024,1024]{1,0:T(8,128)(2,1)}), bf16[512,1024]{1,0:T(8,128)(2,1)}) %reduce-scatter.11.cloned.1.call-update) | async-done | bytes 1048592 | tf_op jit(solution)/shard_map/reduce_scatter | solution.py:152
  246.9 21.4 %all-gather = bf16[16,4,32]{2,1,0:T(4,128)(2,1)S(1)} all-gather(bf16[1,4,32]{2,1,0:T(4,128)(2,1)S(1)} %bitcast.122), channel_id=1, replica_groups=mesh['dp'=16,'tensor'=2] {'dp'}, dimensions={0}, use_global_device_ids=true | all-gather | bytes 4352 | tf_op jit(solution)/shard_map/all_gather | solution.py:118
  268.4 24.0 %all-gather.18.cloned.1.call-done = bf16[1024,2048]{1,0:T(8,128)(2,1)} async-done(((bf16[64,2048]{1,0:T(8,128)(2,1)}), bf16[1024,2048]{1,0:T(8,128)(2,1)}) %all-gather.18.cloned.1.call-update) | async-done | bytes 4194320 | tf_op jit(solution)/shard_map/all_gather | solution.py:111
  292.5 33.7 %all-gather.16.cloned.1.call-done = bf16[1024,1024]{1,0:T(8,128)(2,1)} async-done(((bf16[512,1024]{1,0:T(8,128)(2,1)}), bf16[1024,1024]{1,0:T(8,128)(2,1)}) %all-gather.16.cloned.1.call-update) | async-done | bytes 2097168 | tf_op jit(solution)/shard_map/all_gather | solution.py:165
  326.2 10.9 %fusion.70 = f32[1024,2048]{1,0:T(8,128)} fusion(bf16[1024,1024]{1,0:T(8,128)(2,1)} %all-gather.16.cloned.1.call-done, bf16[1024,2048]{1,0:T(8,128)(2,1)} %all-gather.18.cloned.1.call-done), kind=kOutput, calls=%fused_computation.139 | convolution fusion | flops 4294967296 | bytes 14680064 | tf_op jit(solution)/shard_map/dot_general | solution.py:166
  337.1 24.5 %all-gather.22.cloned.1.call-done = bf16[1024,1024]{1,0:T(8,128)(2,1)} async-done(((bf16[512,1024]{1,0:T(8,128)(2,1)}), bf16[1024,1024]{1,0:T(8,128)(2,1)}) %all-gather.22.cloned.1.call-update) | async-done | bytes 2097168 | tf_op jit(solution)/shard_map/all_gather | solution.py:189
  361.5 53.1 %all-gather.20.cloned.1.call-done = bf16[2048,1024]{0,1:T(8,128)(2,1)} async-done(((bf16[2048,64]{0,1:T(8,128)(2,1)}), bf16[2048,1024]{0,1:T(8,128)(2,1)}) %all-gather.20.cloned.1.call-update) | async-done | bytes 4194320 | tf_op jit(solution)/shard_map/all_gather | solution.py:117
  414.6 13.4 %fusion.69 = (bf16[2048]{0:T(1024)(128)(2,1)}, bf16[1024,2048]{1,0:T(8,128)(2,1)S(1)}) fusion(f32[1024,2048]{1,0:T(8,128)} %fusion.70, f32[2048]{0:T(1024)S(1)} %reshape.303, bf16[1024,1024]{1,0:T(8,128)(2,1)} %all-gather.22.cloned.1.call-done, bf16[2048,1024]{0,1:T(8,128)(2,1)} %all-gather.20.cloned.1.call-done), kind=kOutput, calls=%fused_computation.138 | convolution fusion | flops 4339005440 | bytes 18886656 | tf_op jit(solution)/shard_map/td,fd->tf/dot_general | solution.py:191
  435.8 30.4 %reduce-scatter.15.cloned.1.call-done = bf16[512,1024]{1,0:T(8,128)(2,1)} async-done(((bf16[1024,1024]{1,0:T(8,128)(2,1)}), bf16[512,1024]{1,0:T(8,128)(2,1)}) %reduce-scatter.15.cloned.1.call-update) | async-done | bytes 1048592 | tf_op jit(solution)/shard_map/reduce_scatter | solution.py:198
  474.7 10.3 %convolution_convert_fusion = bf16[2048,1024]{0,1:T(8,128)(2,1)} fusion(bf16[1024,1024]{1,0:T(8,128)(2,1)S(1)} %copy-done.50, f32[1024,2048]{1,0:T(8,128)} %fusion.70, f32[2048]{0:T(1024)S(1)} %reshape.303), kind=kOutput, calls=%fused_computation.23 | convolution fusion | flops 4318035968 | bytes 14688256 | tf_op jit(solution)/shard_map/tf,td->fd/dot_general | solution.py:190
  486.5 8.3 convolution_convert_fusion.1
  495.0 12.5 %all-gather.24.cloned.1.call-done = bf16[1024,1024]{1,0:T(8,128)(2,1)} async-done(((bf16[512,1024]{1,0:T(8,128)(2,1)}), bf16[1024,1024]{1,0:T(8,128)(2,1)}) %all-gather.24.cloned.1.call-update) | async-done | bytes 2097168 | tf_op jit(solution)/shard_map/all_gather | solution.py:211
  515.1 10.8 %multiply_convert_fusion.1 = bf16[8,512,1024]{2,1,0:T(8,128)(2,1)S(1)} fusion(f32[8,512,1024]{2,1,0:T(8,128)} %get-tuple-element.112, bf16[512,8,64]{0,2,1:T(8,128)(2,1)} %bitcast.115, bf16[1024,8,64]{0,2,1:T(8,128)(2,1)} %bitcast.111, f32[8,512]{1,0:T(8,128)} %bitcast.120, f32[8,512]{1,0:T(8,128)} %copy-done.37, pred[512,1024]{1,0:T(8,128)(4,1)} %copy-done.13), kind=kOutput, calls=%fused_computation.1 | convolution fusion | flops 566231040 | bytes 27295744 | tf_op jit(solution)/shard_map/qhd,khd->hqk/dot_general | solution.py:230
  533.5 8.2 fusion.56
  548.7 10.3 %multiply_convert_fusion = bf16[8,512,1024]{2,1,0:T(8,128)(2,1)} fusion(f32[8,512,1024]{2,1,0:T(8,128)S(1)} %bitcast.95, bf16[512,8,64]{0,2,1:T(8,128)(2,1)} %bitcast.113, bf16[1024,8,64]{0,2,1:T(8,128)(2,1)} %bitcast.112, f32[8,512]{1,0:T(8,128)} %bitcast.119, f32[8,512]{1,0:T(8,128)} %copy-done.35, pred[512,1024]{1,0:T(8,128)(4,1)} %copy-done.11), kind=kOutput, calls=%fused_computation | convolution fusion | flops 566231040 | bytes 27295744 | tf_op jit(solution)/shard_map/qhd,khd->hqk/dot_general | solution.py:230
  565.1 6.9 fusion.64
  575.6 6.2 fusion.63
  583.3 7.4 bitcast_convert_fusion
  591.0 11.8 %convolution_convert_fusion.3 = bf16[1024,1024]{1,0:T(8,128)(2,1)} fusion(bf16[2048,1024]{0,1:T(8,128)(2,1)} %all-gather.20.cloned.1.call-done, f32[1024,2048]{1,0:T(8,128)} %fusion.70, f32[2048]{0:T(1024)S(1)} %copy-done.40), kind=kOutput, calls=%fused_computation.80 | convolution fusion | flops 4316987392 | bytes 14688256 | tf_op jit(solution)/shard_map/dot_general | solution.py:170
  602.9 7.6 convolution_convert_fusion.2
  616.2 43.2 %reduce-scatter.23.cloned.1.call-done = bf16[64,2048]{1,0:T(8,128)(2,1)} async-done(((bf16[1024,2048]{1,0:T(8,128)(2,1)}), bf16[64,2048]{1,0:T(8,128)(2,1)}) %reduce-scatter.23.cloned.1.call-update) | async-done | bytes 262160 | tf_op jit(solution)/shard_map/reduce_scatter | solution.py:278
  661.2 58.4 %reduce-scatter.21.cloned.1.call-done = bf16[512,64]{0,1:T(8,128)(2,1)} async-done(((bf16[512,1024]{0,1:T(8,128)(2,1)}), bf16[512,64]{0,1:T(8,128)(2,1)}) %reduce-scatter.21.cloned.1.call-update) | async-done | bytes 65552 | tf_op jit(solution)/shard_map/reduce_scatter | solution.py:299
  721.1 31.5 %reduce-scatter.17.cloned.1.call-done = bf16[512,1024]{1,0:T(8,128)(2,1)} async-done(((bf16[1024,1024]{1,0:T(8,128)(2,1)}), bf16[512,1024]{1,0:T(8,128)(2,1)}) %reduce-scatter.17.cloned.1.call-update) | async-done | bytes 1048592 | tf_op jit(solution)/shard_map/reduce_scatter | solution.py:249
  756.2 61.3 %all-reduce.15 = (bf16[1024]{0:T(1024)(128)(2,1)S(1)}, bf16[1024]{0:T(1024)(128)(2,1)S(1)}, bf16[1024]{0:T(1024)(128)(2,1)S(1)}, bf16[1024]{0:T(1024)(128)(2,1)S...) all-reduce(bf16[1024]{0:T(1024)(128)(2,1)S(1)} %dynamic-update-slic, ...), channel_id=1, replica_groups=mesh['dp'=16,'tensor'=2] {'dp'}, use_global_device_ids=true, to_apply=%add.5 | all-reduce | flops 10240 | bytes 40960
  829.1 27.8 %reduce-scatter.19.cloned.1.call-done = bf16[64,3,512]{2,0,1:T(8,128)(2,1)} async-done(((bf16[1024,3,512]{2,0,1:T(8,128)(2,1)}), bf16[64,3,512]{2,0,1:T(8,128)(2,1)}) %reduce-scatter.19.cloned.1.call-update) | async-done | bytes 196624 | tf_op jit(solution)/shard_map/reduce_scatter | solution.py:275
  (252 shorter events, 117.4 us)
Async XLA Ops:
  7.2 76.6 %copy-start.30 = (s32[1024]{0:T(1024)S(1)}, s32[1024]{0:T(1024)}, u32[]{:S(2)}) copy-start(s32[1024]{0:T(1024)} %param.17) | copy-start | bytes 12292
  7.2 76.9 %copy-start.45 = (bf16[2,8,4]{1,2,0:T(4,128)(2,1)S(1)}, bf16[2,8,4]{1,2,0:T(4,128)(2,1)}, u32[]{:S(2)}) copy-start(bf16[2,8,4]{1,2,0:T(4,128)(2,1)} %param.22) | copy-start | bytes 388
  7.2 95.0 %copy-start.47 = (s32[8]{0:T(128)S(1)}, s32[8]{0:T(128)}, u32[]{:S(2)}) copy-start(s32[8]{0:T(128)} %param.18) | copy-start | bytes 100
  7.2 105.5 %all-gather.10.cloned.1.call-start = ((), (), s32[]{:S(2)}) async-start(), calls=%async_computation.8 | async-start | bytes 3145728 | tf_op jit(solution)/shard_map/all_gather | solution.py:128
  8.7 75.3 %copy-start.31 = (f32[512]{0:T(512)}, f32[512]{0:T(512)S(1)}, u32[]{:S(2)}) copy-start(f32[512]{0:T(512)S(1)} %broadcast_multiply_fusion.5) | copy-start | bytes 6148
  10.4 73.7 %copy-start.33 = (f32[512]{0:T(512)}, f32[512]{0:T(512)S(1)}, u32[]{:S(2)}) copy-start(f32[512]{0:T(512)S(1)} %add_rsqrt_fusion.1) | copy-start | bytes 6148
  82.2 78.0 %all-gather.12.cloned.1.call-start = ((), (), s32[]{:S(2)}) async-start(), calls=%async_computation.9 | async-start | bytes 3342336 | tf_op jit(solution)/shard_map/all_gather | solution.py:110
  82.9 121.1 %all-gather.14.cloned.1.call-start = ((), (), s32[]{:S(2)}) async-start(), calls=%async_computation.10 | async-start | bytes 1114112 | tf_op jit(solution)/shard_map/all_gather | solution.py:116
  83.7 155.9 %reduce-scatter.11.cloned.1.call-start = ((), (), s32[]{:S(2)}) async-start(), calls=%async_computation.11 | async-start | bytes 3145728 | tf_op jit(solution)/shard_map/reduce_scatter | solution.py:152
  103.8 87.2 %copy-start.13 = (pred[512,1024]{1,0:T(8,128)(4,1)}, pred[512,1024]{1,0:T(8,128)(4,1)S(1)}, u32[]{:S(2)}) copy-start(pred[512,1024]{1,0:T(8,128)(4,1)S(1)} %get-tuple-element.103) | copy-start | bytes 1572868
  103.8 95.3 %copy-start.11 = (pred[512,1024]{1,0:T(8,128)(4,1)}, pred[512,1024]{1,0:T(8,128)(4,1)S(1)}, u32[]{:S(2)}) copy-start(pred[512,1024]{1,0:T(8,128)(4,1)S(1)} %get-tuple-element.104) | copy-start | bytes 1572868
  208.6 83.9 %all-gather.18.cloned.1.call-start = ((), (), s32[]{:S(2)}) async-start(), calls=%async_computation.13 | async-start | bytes 4456448 | tf_op jit(solution)/shard_map/all_gather | solution.py:111
  209.2 117.0 %all-gather.16.cloned.1.call-start = ((), (), s32[]{:S(2)}) async-start(), calls=%async_computation.12 | async-start | bytes 3145728 | tf_op jit(solution)/shard_map/all_gather | solution.py:165
  209.3 35.6 %copy-start.15 = (bf16[512,1024]{1,0:T(8,128)(2,1)S(1)}, bf16[512,1024]{1,0:T(8,128)(2,1)}, u32[]{:S(2)}) copy-start(bf16[512,1024]{1,0:T(8,128)(2,1)} %param.31) | copy-start | bytes 3145732
  244.8 116.8 %all-gather.22.cloned.1.call-start = ((), (), s32[]{:S(2)}) async-start(), calls=%async_computation.16 | async-start | bytes 3145728 | tf_op jit(solution)/shard_map/all_gather | solution.py:189
  244.9 224.4 %copy-start.42 = (pred[512]{0:T(512)(128)(4,1)}, pred[512]{0:T(512)(128)(4,1)S(1)}, u32[]{:S(2)}) copy-start(pred[512]{0:T(512)(128)(4,1)S(1)} %dynamic_slice.3) | copy-start | bytes 1540
  246.1 168.5 %all-gather.20.cloned.1.call-start = ((), (), s32[]{:S(2)}) async-start(), calls=%async_computation.14 | async-start | bytes 4456448 | tf_op jit(solution)/shard_map/all_gather | solution.py:117
  246.9 219.4 %reduce-scatter.15.cloned.1.call-start = ((), (), s32[]{:S(2)}) async-start(), calls=%async_computation.17 | async-start | bytes 3145728 | tf_op jit(solution)/shard_map/reduce_scatter | solution.py:198
  268.4 206.2 %copy-start.39 = (f32[2048]{0:T(1024)}, f32[2048]{0:T(1024)S(1)}, u32[]{:S(2)}) copy-start(f32[2048]{0:T(1024)S(1)} %reshape.303) | copy-start | bytes 24580
  435.8 71.7 %all-gather.24.cloned.1.call-start = ((), (), s32[]{:S(2)}) async-start(), calls=%async_computation.18 | async-start | bytes 3145728 | tf_op jit(solution)/shard_map/all_gather | solution.py:211
  474.2 140.2 %reduce-scatter.25.cloned.1.call-start = ((), (), s32[]{:S(2)}) async-start(), calls=%async_computation.23 | async-start | bytes 4456448 | tf_op jit(solution)/shard_map/reduce_scatter | solution.py:302
  485.0 174.5 %reduce-scatter.23.cloned.1.call-start = ((), (), s32[]{:S(2)}) async-start(), calls=%async_computation.22 | async-start | bytes 4456448 | tf_op jit(solution)/shard_map/reduce_scatter | solution.py:278
  494.9 224.7 %reduce-scatter.21.cloned.1.call-start = ((), (), s32[]{:S(2)}) async-start(), calls=%async_computation.21 | async-start | bytes 1114112 | tf_op jit(solution)/shard_map/reduce_scatter | solution.py:299
  559.0 193.5 %reduce-scatter.17.cloned.1.call-start = ((), (), s32[]{:S(2)}) async-start(), calls=%async_computation.19 | async-start | bytes 3145728 | tf_op jit(solution)/shard_map/reduce_scatter | solution.py:249
  590.7 234.1 %reduce-scatter.13.cloned.1.call-start = ((), (), s32[]{:S(2)}) async-start(), calls=%async_computation.15 | async-start | bytes 3145728 | tf_op jit(solution)/shard_map/reduce_scatter | solution.py:169
  602.9 253.9 %reduce-scatter.19.cloned.1.call-start = ((), (), s32[]{:S(2)}) async-start(), calls=%async_computation.20 | async-start | bytes 3342336 | tf_op jit(solution)/shard_map/reduce_scatter | solution.py:275
  610.5 143.5 %copy-start.29 = (f32[1024]{0:T(1024)S(1)}, f32[1024]{0:T(1024)}, u32[]{:S(2)}) copy-start(f32[1024]{0:T(1024)} %copy-done.28) | copy-start | bytes 12292
  610.5 143.5 %copy-start.32 = (f32[512]{0:T(512)S(1)}, f32[512]{0:T(512)}, u32[]{:S(2)}) copy-start(f32[512]{0:T(512)} %copy-done.31) | copy-start | bytes 6148
  610.6 143.5 %copy-start.34 = (f32[512]{0:T(512)S(1)}, f32[512]{0:T(512)}, u32[]{:S(2)}) copy-start(f32[512]{0:T(512)} %copy-done.33) | copy-start | bytes 6148
  610.6 145.7 %copy-start.41 = (bf16[1024]{0:T(1024)(128)(2,1)S(1)}, bf16[1024]{0:T(1024)(128)(2,1)}, u32[]{:S(2)}) copy-start(bf16[1024]{0:T(1024)(128)(2,1)} %get-tuple-element.56) | copy-start | bytes 6148
  610.6 214.2 %copy-start.4 = (bf16[512,1024]{1,0:T(8,128)(2,1)S(1)}, bf16[512,1024]{1,0:T(8,128)(2,1)}, u32[]{:S(2)}) copy-start(bf16[512,1024]{1,0:T(8,128)(2,1)} %reduce-scatter.11.cloned.1.call-done) | copy-start | bytes 3145732
  610.6 214.2 %copy-start.43 = (pred[512]{0:T(512)(128)(4,1)S(1)}, pred[512]{0:T(512)(128)(4,1)}, u32[]{:S(2)}) copy-start(pred[512]{0:T(512)(128)(4,1)} %copy-done.42) | copy-start | bytes 1540
  (42 other events, 368.8 us)
Sparse Core Ops, SparseCore 0:
  82.3 30.3 all-gather.9
  114.9 45.1 all-gather.11
  162.3 36.7 all-gather.13
  208.7 30.8 reduce-scatter.10
  241.8 50.5 all-gather.17
  294.5 31.6 all-gather.15
  328.4 33.1 all-gather.21
  363.9 50.7 all-gather.19
  435.9 30.3 reduce-scatter.14
  474.3 33.1 all-gather.23
  511.3 72.3 reduce-scatter.24
  587.9 71.4 reduce-scatter.22
  663.0 56.4 reduce-scatter.20
  721.8 30.7 reduce-scatter.16
  754.7 31.8 reduce-scatter.12
  790.7 66.1 reduce-scatter.18
where the time goes:
time: 870 us; the launch traced here: 865 us
  waiting for transfers between devices  429 us (49%)
  matrix products  173 us (20%)
  blocking collectives  169 us (19%)
  other arithmetic  53 us (6%)
  local copies, waits for them, and re-layouts  23.1 us (3%)
  between operations  17.1 us (2%)
    unnamed x2, blocking collectives  124 us
    reduce_scatter x1, waiting for transfers between devices, local(): lax.psum_scatter(grad_out_weight.astype(jnp.bfloat16), 'dp', scatter_dime...  58.4 us
    all_gather x1, waiting for transfers between devices, local(): lax.all_gather(down_weight, 'dp', axis=1, tiled=True)  53.1 us
    all_gather x1, waiting for transfers between devices, local(): lax.all_gather(qkv_weight, 'dp', axis=0, tiled=True)  47.4 us
    reduce_scatter x1, waiting for transfers between devices, local(): lax.psum_scatter(grad_up_weight.astype(jnp.bfloat16), 'dp', scatter_dimen...  43.2 us
    all_gather x1, waiting for transfers between devices, local(): a2_all = lax.all_gather(a2_full.astype(bf16), 'tensor', axis=0, tiled=True)  33.7 us
    reduce_scatter x1, waiting for transfers between devices, local(): lax.psum_scatter(jnp.einsum('tck,dck->td', piece, w_qkv, preferred_elemen...  31.5 us
    reduce_scatter x1, waiting for transfers between devices, local(): lax.psum_scatter(jnp.einsum('tf,df->td', piece, w_up, preferred_element_t...  30.4 us
  transfers between devices with their start and end apart: 16, of which 13 were waited for; matrix products, arithmetic and copies ran while one was open for 23% of the time, Pallas kernels for 0%

commit v1 on v0

v1 whole, which is shorter than its diff:
```python
import functools

import jax
import jax.numpy as jnp
from jax import lax
from jax.experimental import pallas as pl
from jax.experimental.pallas import tpu as pltpu
from jax.sharding import PartitionSpec as P

HD = 64


epsilon = 1e-05
masked_fill = -1e30
gelu_root = 0.7978845608028654
gelu_cubic = 0.044715


def layer_norm(hidden, gain, shift):
    center = hidden - jnp.mean(hidden, axis=-1, keepdims=True)
    inverse = lax.rsqrt(jnp.mean(center * center, axis=-1, keepdims=True) + epsilon)
    normed = center * inverse
    return (normed * gain + shift, normed, inverse)


def norm_back(upstream, gain, normed, inverse):
    scaled = upstream * gain
    return inverse * (
        scaled
        - jnp.mean(scaled, axis=-1, keepdims=True)
        - normed * jnp.mean(scaled * normed, axis=-1, keepdims=True)
    )


def gelu_value(inputs):
    tangent = jnp.tanh(gelu_root * (inputs + gelu_cubic * inputs * inputs * inputs))
    return 0.5 * inputs * (1.0 + tangent)


def gelu_slope(inputs):
    tangent = jnp.tanh(gelu_root * (inputs + gelu_cubic * inputs * inputs * inputs))
    return 0.5 * (1.0 + tangent) + 0.5 * inputs * (1.0 - tangent * tangent) * gelu_root * (
        1.0 + 3.0 * gelu_cubic * inputs * inputs
    )


def live_slots(slot_seq, seq_len):
    numbers = seq_len.shape[0]
    onehot = (slot_seq[:, None] == jnp.arange(numbers, dtype=jnp.int32)[None, :]).astype(jnp.int32)
    counts = jnp.sum(onehot, axis=0, dtype=jnp.int32)
    first_slot = jnp.cumsum(counts, dtype=jnp.int32) - counts
    run_start = jnp.sum(onehot * first_slot[None, :], axis=1, dtype=jnp.int32)
    run_length = jnp.sum(onehot * seq_len[None, :], axis=1, dtype=jnp.int32)
    places = jnp.arange(slot_seq.shape[0], dtype=jnp.int32) - run_start
    return places < run_length


LANES = 128
NT = (((1,), (1,)), ((), ()))
TN = (((0,), (0,)), ((), ()))
f32 = jnp.float32
bf16 = jnp.bfloat16


def half_mask(half):
    lane = lax.broadcasted_iota(jnp.int32, (1, LANES), 1)
    return (lane >= HD) == (half == 1)


def block_allowed(seq_col_ref, key_row_ref, first, rows, width):
    query_index = first + lax.broadcasted_iota(jnp.int32, (rows, width), 0)
    key_index = lax.broadcasted_iota(jnp.int32, (rows, width), 1)
    same = seq_col_ref[first : first + rows, :] == key_row_ref[:, :width]
    return same & (key_index <= query_index)


def attention_kernel(rows, seq_col_ref, key_row_ref, q_ref, k_ref, v_ref, o_ref, lse_ref):
    slots = q_ref.shape[0]
    value_sum = jnp.sum(v_ref[...].astype(f32), axis=0, keepdims=True)
    for first in range(0, slots, rows):
        width = first + rows
        allowed = block_allowed(seq_col_ref, key_row_ref, first, rows, width)
        out = jnp.zeros((rows, LANES), f32)
        tops = []
        for half in range(2):
            mask = half_mask(half)
            query = jnp.where(mask, q_ref[first:width, :], 0)
            scores = lax.dot_general(
                query, k_ref[:width, :], NT, preferred_element_type=f32
            ) * HD ** (-0.5)
            scores = jnp.where(allowed, scores, masked_fill)
            top = jnp.max(scores, axis=-1, keepdims=True)
            shifted = jnp.exp(scores - top)
            total = jnp.sum(shifted, axis=-1, keepdims=True)
            log_total = top + jnp.log(total)
            probs = (shifted * (1.0 / total)).astype(bf16)
            value = jnp.where(mask, v_ref[:width, :], 0)
            part = jnp.dot(probs, value, preferred_element_type=f32)
            part = jnp.where(top < 0.1 * masked_fill, jnp.where(mask, value_sum, 0.0), part)
            out = out + part
            lse_ref[0, first:width, half : half + 1] = log_total
        o_ref[first:width, :] = out.astype(bf16)


def attention(qkv, seq_col, key_row, pairs):
    slots = qkv.shape[0]
    rows = min(256, slots)
    column = lambda part: pl.BlockSpec((slots, LANES), lambda i: (0, part * pairs + i))
    return pl.pallas_call(
        functools.partial(attention_kernel, rows),
        grid=(pairs,),
        in_specs=[
            pl.BlockSpec((slots, 1), lambda i: (0, 0)),
            pl.BlockSpec((1, slots), lambda i: (0, 0)),
            column(0),
            column(1),
            column(2),
        ],
        out_specs=[
            pl.BlockSpec((slots, LANES), lambda i: (0, i)),
            pl.BlockSpec((1, slots, 2), lambda i: (i, 0, 0)),
        ],
        out_shape=[
            jax.ShapeDtypeStruct((slots, pairs * LANES), bf16),
            jax.ShapeDtypeStruct((pairs, slots, 2), f32),
        ],
        compiler_params=pltpu.CompilerParams(vmem_limit_bytes=40 * 1024 * 1024),
        cost_estimate=pl.CostEstimate(
            flops=pairs * slots * slots * 512,
            bytes_accessed=pairs * slots * LANES * 12,
            transcendentals=pairs * slots * slots,
        ),
        name="attention",
    )(seq_col, key_row, qkv, qkv, qkv)


def attention_back_kernel(
    rows,
    seq_col_ref,
    key_row_ref,
    q_ref,
    k_ref,
    v_ref,
    o_ref,
    lse_ref,
    do_ref,
    dq_ref,
    dk_ref,
    dv_ref,
    bias_ref,
    dk_sum,
    dv_sum,
):
    slots = q_ref.shape[0]
    dk_sum[...] = jnp.zeros_like(dk_sum)
    dv_sum[...] = jnp.zeros_like(dv_sum)
    dq_total = jnp.zeros((1, LANES), f32)
    for first in range(0, slots, rows):
        width = first + rows
        allowed = block_allowed(seq_col_ref, key_row_ref, first, rows, width)
        product = do_ref[first:width, :].astype(f32) * o_ref[first:width, :].astype(f32)
        dq = jnp.zeros((rows, LANES), f32)
        for half in range(2):
            mask = half_mask(half)
            query = jnp.where(mask, q_ref[first:width, :], 0)
            key = jnp.where(mask, k_ref[:width, :], 0)
            upstream = jnp.where(mask, do_ref[first:width, :], 0)
            delta = jnp.sum(jnp.where(mask, product, 0.0), axis=-1, keepdims=True)
            scores = lax.dot_general(query, key, NT, preferred_element_type=f32) * HD ** (-0.5)
            scores = jnp.where(allowed, scores, masked_fill)
            probs = jnp.exp(scores - lse_ref[0, first:width, half : half + 1])
            grad_probs = lax.dot_general(
                upstream, v_ref[:width, :], NT, preferred_element_type=f32
            )
            grad_scores = (probs * ((grad_probs - delta) * HD ** (-0.5))).astype(bf16)
            dq = dq + jnp.dot(grad_scores, key, preferred_element_type=f32)
            dk_sum[:width, :] += lax.dot_general(
                grad_scores, query, TN, preferred_element_type=f32
            )
            dv_sum[:width, :] += lax.dot_general(
                probs.astype(bf16), upstream, TN, preferred_element_type=f32
            )
        dq_ref[first:width, :] = dq.astype(bf16)
        dq_total = dq_total + jnp.sum(dq, axis=0, keepdims=True)
    dk_ref[...] = dk_sum[...].astype(bf16)
    dv_ref[...] = dv_sum[...].astype(bf16)
    bias_ref[0:1, :] = dq_total
    bias_ref[1:2, :] = jnp.sum(dv_sum[...], axis=0, keepdims=True)


def attention_back(qkv, seq_col, key_row, heads, lse, grad_heads, pairs):
    slots = qkv.shape[0]
    rows = min(256, slots)
    column = lambda part: pl.BlockSpec((slots, LANES), lambda i: (0, part * pairs + i))
    return pl.pallas_call(
        functools.partial(attention_back_kernel, rows),
        grid=(pairs,),
        in_specs=[
            pl.BlockSpec((slots, 1), lambda i: (0, 0)),
            pl.BlockSpec((1, slots), lambda i: (0, 0)),
            column(0),
            column(1),
            column(2),
            column(0),
            pl.BlockSpec((1, slots, 2), lambda i: (i, 0, 0)),
            column(0),
        ],
        out_specs=[column(0), column(0), column(0), pl.BlockSpec((2, LANES), lambda i: (0, i))],
        out_shape=[jax.ShapeDtypeStruct((slots, pairs * LANES), bf16)] * 3
        + [jax.ShapeDtypeStruct((2, pairs * LANES), f32)],
        scratch_shapes=[pltpu.VMEM((slots, LANES), f32), pltpu.VMEM((slots, LANES), f32)],
        compiler_params=pltpu.CompilerParams(vmem_limit_bytes=40 * 1024 * 1024),
        cost_estimate=pl.CostEstimate(
            flops=pairs * slots * slots * 1280,
            bytes_accessed=pairs * slots * LANES * 20,
            transcendentals=pairs * slots * slots,
        ),
        name="attention_back",
    )(seq_col, key_row, qkv, qkv, qkv, heads, lse, grad_heads)


def swap(block):
    return lax.ppermute(block, "tensor", [(0, 1), (1, 0)])


def gather_rows(block):
    if lax.axis_size("tensor") != 2:
        return lax.all_gather(block, "tensor", axis=0, tiled=True)
    other = swap(block)
    return jnp.where(
        lax.axis_index("tensor") == 0,
        jnp.concatenate([block, other], axis=0),
        jnp.concatenate([other, block], axis=0),
    )


def own_sum(left, right, own_rows):
    product = lambda rows: lax.dot_general(rows, right, NT, preferred_element_type=f32).astype(bf16)
    if lax.axis_size("tensor") != 2:
        total = product(left)
        return (
            lax.psum_scatter(total, "tensor", scatter_dimension=0, tiled=True).astype(f32),
            total,
        )
    me = lax.axis_index("tensor")
    send = product(lax.dynamic_slice_in_dim(left, (1 - me) * own_rows, own_rows))
    arrived = swap(send)
    keep = product(lax.dynamic_slice_in_dim(left, me * own_rows, own_rows))
    return keep.astype(f32) + arrived.astype(f32), (send, keep)


def as_columns(vector, rows):
    flat = vector.reshape(-1)
    columns = -(-flat.shape[0] // rows)
    return jnp.pad(flat, (0, columns * rows - flat.shape[0])).reshape(rows, columns)


def pad_columns(array):
    return jnp.pad(array, ((0, 0), (0, -array.shape[1] % LANES)))


def scatter_groups(array):
    return lax.psum_scatter(array, "dp", scatter_dimension=0, tiled=True).astype(f32)


def local(
    tokens,
    slot_seq,
    seq_len,
    ln1_gain,
    ln1_shift,
    qkv_weight,
    qkv_bias,
    out_weight,
    out_bias,
    ln2_gain,
    ln2_shift,
    up_weight,
    up_bias,
    down_weight,
    down_bias,
    cotangent,
):
    own_rows, width = tokens.shape
    slots = slot_seq.shape[0]
    shard = ln1_gain.shape[0]
    groups = lax.axis_size("dp")
    me = lax.axis_index("tensor")
    here = qkv_weight.shape[2]
    hidden = up_weight.shape[1]
    heads_here = here // HD
    pairs = here // LANES

    vectors = jnp.stack([ln1_gain, ln1_shift, out_bias, ln2_gain, ln2_shift, down_bias], axis=1)
    up_bias_columns = as_columns(up_bias, shard)
    qkv_bias_columns = as_columns(qkv_bias, shard)
    small = pad_columns(
        jnp.concatenate([vectors, up_bias_columns, qkv_bias_columns], axis=1)
    )
    first_piece = jnp.concatenate(
        [qkv_weight.reshape(shard, 3 * here), out_weight.T, small], axis=1
    )
    first_all = lax.all_gather(first_piece, "dp", axis=0, tiled=True)
    second_all = lax.all_gather(
        jnp.concatenate([up_weight, down_weight.T], axis=1), "dp", axis=0, tiled=True
    )
    w_qkv = first_all[:, : 3 * here]
    w_out_t = first_all[:, 3 * here : 4 * here]
    w_up = second_all[:, :hidden]
    w_down_t = second_all[:, hidden:]
    small_all = first_all[:, 4 * here :].astype(f32)
    gain_one, shift_one, bias_out, gain_two, shift_two, bias_down = (
        small_all[:, i] for i in range(6)
    )

    def unpack(start, columns, shape, axis):
        flat = small_all[:, start : start + columns].reshape(groups, shard * columns)
        count = 1
        for size in shape:
            count *= size
        parts = flat[:, :count].reshape((groups,) + shape)
        parts = jnp.moveaxis(parts, 0, axis)
        return parts.reshape(shape[:axis] + (groups * shape[axis],) + shape[axis + 1 :])

    up_columns = up_bias_columns.shape[1]
    bias_up = unpack(6, up_columns, up_bias.shape, 1).reshape(-1)
    bias_rows = unpack(6 + up_columns, qkv_bias_columns.shape[1], qkv_bias.shape, 2).reshape(
        2, here
    )
    bias_qkv = jnp.concatenate([bias_rows[0], jnp.zeros_like(bias_rows[0]), bias_rows[1]])

    live = live_slots(slot_seq, seq_len)
    own_live = lax.dynamic_slice_in_dim(live, me * own_rows, own_rows)
    seq_col = slot_seq[:, None]
    key_row = jnp.where(live, slot_seq, -1)[None, :]

    tokens_all = gather_rows(tokens)
    cotangent_all = gather_rows(cotangent)
    grad_h2_all = jnp.where(live[:, None], cotangent_all, jnp.zeros_like(cotangent_all))

    a1_full, normed_one_all, _ = layer_norm(tokens_all.astype(f32), gain_one, shift_one)
    a1_all = a1_full.astype(bf16)
    qkv = (jnp.dot(a1_all, w_qkv, preferred_element_type=f32) + bias_qkv).astype(bf16)
    heads, lse = attention(qkv, seq_col, key_row, pairs)
    attn, _ = own_sum(heads, w_out_t, own_rows)
    inputs = tokens.astype(f32)
    hidden_one = inputs + attn + bias_out
    a2_full, normed_two, inverse_two = layer_norm(hidden_one, gain_two, shift_two)
    a2_all = gather_rows(a2_full.astype(bf16))
    pre = jnp.dot(a2_all, w_up, preferred_element_type=f32) + bias_up
    act = gelu_value(pre).astype(bf16)
    grad_down_weight_t = lax.dot_general(grad_h2_all, act, TN, preferred_element_type=f32)
    grad_pre = jnp.dot(grad_h2_all, w_down_t, preferred_element_type=f32) * gelu_slope(pre)
    grad_up_bias = jnp.sum(grad_pre, axis=0)
    grad_pre_b = grad_pre.astype(bf16)
    grad_a2, _ = own_sum(grad_pre_b, w_up, own_rows)
    grad_up_weight = lax.dot_general(a2_all, grad_pre_b, TN, preferred_element_type=f32)
    second_sum = scatter_groups(
        jnp.concatenate([grad_up_weight.astype(bf16), grad_down_weight_t.astype(bf16)], axis=1)
    )

    mlp, _ = own_sum(act, w_down_t, own_rows)
    output = jnp.where(own_live[:, None], hidden_one + mlp + bias_down, 0.0)

    grad_h2 = jnp.where(own_live[:, None], cotangent.astype(f32), 0.0)
    grad_down_bias = jnp.sum(grad_h2, axis=0)
    grad_ln2_gain = jnp.sum(grad_a2 * normed_two, axis=0)
    grad_ln2_shift = jnp.sum(grad_a2, axis=0)
    grad_h1 = grad_h2 + norm_back(grad_a2, gain_two, normed_two, inverse_two)
    grad_out_bias = jnp.sum(grad_h1, axis=0)
    grad_h1_all = gather_rows(grad_h1.astype(bf16))
    grad_heads = jnp.dot(grad_h1_all, w_out_t, preferred_element_type=f32).astype(bf16)
    grad_out_weight_t = lax.dot_general(grad_h1_all, heads, TN, preferred_element_type=f32)
    dq, dk, dv, grad_qkv_bias = attention_back(
        qkv, seq_col, key_row, heads, lse, grad_heads, pairs
    )
    grad_qkv = jnp.concatenate([dq, dk, dv], axis=1)
    grad_a1, parts = own_sum(grad_qkv, w_qkv, own_rows)
    if lax.axis_size("tensor") == 2:
        send, keep = (part.astype(f32) for part in parts)
        rows_at = lambda place: lax.dynamic_slice_in_dim(normed_one_all, place * own_rows, own_rows)
        grad_ln1_gain = jnp.sum(send * rows_at(1 - me) + keep * rows_at(me), axis=0)
        grad_ln1_shift = jnp.sum(send + keep, axis=0)
    else:
        grad_ln1_gain = jnp.sum(parts.astype(f32) * normed_one_all, axis=0)
        grad_ln1_shift = jnp.sum(parts.astype(f32), axis=0)
    grad_qkv_weight = lax.dot_general(a1_all, grad_qkv, TN, preferred_element_type=f32)

    def pack(gradient, shape, axis):
        parts = gradient.reshape(shape[:axis] + (groups, shape[axis]) + shape[axis + 1 :])
        flat = jnp.moveaxis(parts, axis, 0).reshape(groups, -1)
        columns = -(-flat.shape[1] // shard)
        flat = jnp.pad(flat, ((0, 0), (0, columns * shard - flat.shape[1])))
        return flat.reshape(groups * shard, columns)

    grad_vectors = jnp.stack(
        [
            grad_ln1_gain,
            grad_ln1_shift,
            grad_out_bias,
            grad_ln2_gain,
            grad_ln2_shift,
            grad_down_bias,
        ],
        axis=1,
    )
    grad_small = pad_columns(
        jnp.concatenate(
            [
                grad_vectors,
                pack(grad_up_bias, up_bias.shape, 1),
                pack(grad_qkv_bias, qkv_bias.shape, 2),
            ],
            axis=1,
        )
    )
    first_sum = scatter_groups(
        jnp.concatenate(
            [
                grad_qkv_weight.astype(bf16),
                grad_out_weight_t.astype(bf16),
                grad_small.astype(bf16),
            ],
            axis=1,
        )
    )
    normed_one, inverse_one = layer_norm(inputs, gain_one, shift_one)[1:]
    grad_tokens = grad_h1 + norm_back(grad_a1, gain_one, normed_one, inverse_one)

    small_sum = first_sum[:, 4 * here :]
    vector_sum = small_sum[:, :6].T
    if lax.axis_size("tensor") == 2:
        vector_sum = vector_sum + swap(vector_sum)
    else:
        vector_sum = lax.psum(vector_sum, "tensor")
    up_bias_sum = small_sum[:, 6 : 6 + up_columns].reshape(-1)[: up_bias.size]
    qkv_columns = qkv_bias_columns.shape[1]
    qkv_bias_sum = small_sum[:, 6 + up_columns : 6 + up_columns + qkv_columns].reshape(-1)
    return (
        output,
        grad_tokens,
        vector_sum[0],
        vector_sum[1],
        first_sum[:, : 3 * here].reshape(shard, 3, here),
        qkv_bias_sum[: qkv_bias.size].reshape(qkv_bias.shape),
        first_sum[:, 3 * here : 4 * here].T,
        vector_sum[2],
        vector_sum[3],
        vector_sum[4],
        second_sum[:, :hidden],
        up_bias_sum.reshape(up_bias.shape),
        second_sum[:, hidden:].T,
        vector_sum[5],
    )


def solution(mesh):
    placed = (
        P(("dp", "tensor"), None),
        P("dp"),
        P("dp"),
        P("dp"),
        P("dp"),
        P("dp", None, "tensor"),
        P(None, "tensor", "dp"),
        P("tensor", "dp"),
        P("dp"),
        P("dp"),
        P("dp"),
        P("dp", "tensor"),
        P("tensor", "dp"),
        P("tensor", "dp"),
        P("dp"),
        P(("dp", "tensor"), None),
    )
    return jax.shard_map(
        local,
        mesh=mesh,
        in_specs=placed,
        out_specs=(
            P(("dp", "tensor"), None),
            P(("dp", "tensor"), None),
            P("dp"),
            P("dp"),
            P("dp", None, "tensor"),
            P(None, "tensor", "dp"),
            P("tensor", "dp"),
            P("dp"),
            P("dp"),
            P("dp"),
            P("dp", "tensor"),
            P("tensor", "dp"),
            P("tensor", "dp"),
            P("dp"),
        ),
        check_vma=False,
    )
```

time: 870 us -> 520 us (0.60)
  blocking collectives: 169 us -> 0 us
  waiting for transfers between devices: 429 us -> 269 us
  matrix products: 173 us -> 99.9 us
  Pallas kernels: 0 us -> 40 us
  other arithmetic: 53 us -> 34.4 us
  local copies, waits for them, and re-layouts: 23.1 us -> 38.4 us
  starting transfers between devices: 1.52 us -> 14.6 us
    all_gather x8 -> x2, waiting for transfers between devices: 204 us -> 23.3 us  [the longest x1 23.3 us: local(): first_all = lax.all_gather(first_piece, 'dp', axis=0, tiled=True)]
    ppermute x0 -> x9, waiting for transfers between devices: none -> 138 us  [swap(): return lax.ppermute(block, 'tensor', [(0, 1), (1, 0)])]
    unnamed x2 -> x0, blocking collectives: 124 us -> none
    reduce_scatter x8 -> x2, waiting for transfers between devices: 222 us -> 108 us  [scatter_groups(): lax.psum_scatter(array, 'dp', scatter_dimension=0, tiled=True).astype(f32)]
    dot_general x24 -> x16, matrix products: 173 us -> 99.9 us  [the longest x8 32.1 us: own_sum(): lax.dot_general(rows, right, NT, preferred_element_type=f32).astype(bf16)]
    pallas_call x0 -> x2, Pallas kernels: none -> 40 us  [the longest x1 21.7 us: attention_back(): pl.pallas_call(functools.partial(attention_back_kernel, rows), grid=(pair...]
    all_gather x2 -> x0, blocking collectives: 39.1 us -> none  [the longest x1 21.4 us: local(): lax.all_gather(up_bias, 'dp', axis=1, tiled=True)]
    reduce_sum x8 -> x0, other arithmetic: 23.1 us -> none  [the longest x1 13.6 us: local(): jnp.sum(jnp.exp(scores - top), axis=-1, keepdims=True)]
  transfers between devices with their start and end apart: 16 -> 13, of which waited for: 13 -> 11; matrix products, arithmetic and copies ran while one was open for 23% -> 22% of each run, Pallas kernels for 0% -> 4%
where the time goes in v1:
time: 520 us; the launch traced here: 511 us
  waiting for transfers between devices  269 us (52%)
  matrix products  99.9 us (19%)
  Pallas kernels  40 us (8%)
  local copies, waits for them, and re-layouts  38.4 us (7%)
  other arithmetic  34.4 us (7%)
  between operations  14.8 us (3%)
  starting transfers between devices  14.6 us (3%)
    ppermute x9, waiting for transfers between devices, swap(): return lax.ppermute(block, 'tensor', [(0, 1), (1, 0)])  138 us
    reduce_scatter x2, waiting for transfers between devices, scatter_groups(): lax.psum_scatter(array, 'dp', scatter_dimension=0, tiled=True).astype(f32)  108 us
    dot_general x8, matrix products, own_sum(): lax.dot_general(rows, right, NT, preferred_element_type=f32).astype(bf16)  32.1 us
    all_gather x1, waiting for transfers between devices, local(): first_all = lax.all_gather(first_piece, 'dp', axis=0, tiled=True)  23.3 us
    pallas_call x1, Pallas kernels, attention_back(): pl.pallas_call(functools.partial(attention_back_kernel, rows), grid=(pair...  21.7 us
    pallas_call x1, Pallas kernels, attention(): pl.pallas_call(functools.partial(attention_kernel, rows), grid=(pairs,),...  18.3 us
    ppermute x9, starting transfers between devices, swap(): return lax.ppermute(block, 'tensor', [(0, 1), (1, 0)])  14.3 us
    dot_general x1, matrix products, local(): jnp.dot(grad_h2_all, w_down_t, preferred_element_type=f32) * gelu_slope(pre)  13.6 us
  transfers between devices with their start and end apart: 13, of which 11 were waited for; matrix products, arithmetic and copies ran while one was open for 22% of the time, Pallas kernels for 4%

profile of v1, /device:TPU:0, one launch (start us, length us, event | category | flops | bytes accessed | tf_op | source)
XLA Modules:
  0.0 511.2 jit_solution(11440260259142893000)
XLA Ops:
  18.3 3.0 collective-permute-start
  23.5 21.2 %collective-permute-done = bf16[512,1024]{1,0:T(8,128)(2,1)S(1)} collective-permute-done((bf16[512,1024]{1,0:T(8,128)(2,1)}, bf16[512,1024]{1,0:T(8,128)(2,1)S(1)}, u32[]{:S(2)}, u32[]{:S(2)}) %collective-permute-start) | collective-permute-done | bytes 1048608 | tf_op jit(solution)/shard_map/ppermute | solution.py:223
  47.9 23.3 %all-gather.3.cloned.1.call-done = bf16[1024,2176]{1,0:T(8,128)(2,1)} async-done(((bf16[64,2176]{1,0:T(8,128)(2,1)}), bf16[1024,2176]{1,0:T(8,128)(2,1)}) %all-gather.3.cloned.1.call-update) | async-done | bytes 4456464 | tf_op jit(solution)/shard_map/all_gather | solution.py:303
  75.2 7.0 %add_convert_fusion.q_ref.k_ref.v_ref = bf16[1024,1536]{1,0:T(8,128)(2,1)S(1)} fusion(f32[1536]{0:T(1024)S(1)} %pad_maximum_fusion.2, bf16[1024,2176]{1,0:T(8,128)(2,1)} %all-gather.3.cloned.1.call-done, f32[1024]{0:T(1024)S(1)} %get-tuple-element.97, f32[1024]{0:T(1024)S(1)} %get-tuple-element.98, f32[1024]{0:T(1024)S(1)} %add_rsqrt_fusion, ...), kind=kOutput, calls=%fused_computation.12 | convolution fusion | flops 3240099840 | bytes 8411137 | tf_op jit(solution)/shard_map/dot_general | solution.py:343
  82.2 18.3 %attention.1 = (bf16[1024,512]{1,0:T(8,128)(2,1)S(1)}, f32[4,1024,2]{2,1,0:T(8,128)S(1)}) custom-call(s32[1024,1]{1,0:T(8,128)S(1)} %copy-done, s32[1,1024]{1,0:T(1,128)S(1)} %bitcast.41, bf16[1024,1536]{1,0:T(8,128)(2,1)S(1)} %add_convert_fusion.q_ref.k_ref.v_ref, bf16[1024,1536]{1,0:T(8,128)(2,1)S(1)} %add_convert_fusion.q_ref.k_ref.v_ref, ...), custom_call_target="tpu_custom_call" | custom-call | flops 2147483648 | bytes 6291456 | tf_op jit(solution)/shard_map/attention/pallas_call | solution.py:109
  107.2 24.2 %collective-permute-done.1 = bf16[512,1024]{1,0:T(8,128)(2,1)} collective-permute-done((bf16[512,1024]{1,0:T(8,128)(2,1)}, bf16[512,1024]{1,0:T(8,128)(2,1)}, u32[]{:S(2)}, u32[]{:S(2)}) %collective-permute-start.1) | collective-permute-done | bytes 1048608 | tf_op jit(solution)/shard_map/ppermute | solution.py:223
  131.4 3.2 fusion.114
  143.5 20.2 %collective-permute-done.2 = bf16[512,1024]{1,0:T(8,128)(2,1)} collective-permute-done((bf16[512,1024]{1,0:T(8,128)(2,1)}, bf16[512,1024]{1,0:T(8,128)(2,1)}, u32[]{:S(2)}, u32[]{:S(2)}) %collective-permute-start.2) | collective-permute-done | bytes 1048608 | tf_op jit(solution)/shard_map/ppermute | solution.py:223
  163.7 12.4 %multiply_convert_fusion = (bf16[1024,2048]{1,0:T(8,128)(2,1)}, f32[1024,2048]{1,0:T(8,128)}) fusion(f32[2048]{0:T(1024)S(1)} %add.173, bf16[1024,4096]{1,0:T(8,128)(2,1)} %all-gather.5.cloned.1.call-done, bf16[512,1024]{1,0:T(8,128)(2,1)} %collective-permute-done.2, bf16[512,1024]{1,0:T(8,128)(2,1)} %add_convert_fusion.2, pred[]{:T(512)S(6)} %eq.22), kind=kOutput, calls=%fused_computation.11 | convolution fusion | flops 4325376000 | bytes 18882560 | tf_op jit(solution)/shard_map/dot_general | solution.py:350
  176.1 8.6 %collective-permute-done.4 = bf16[512,1024]{1,0:T(8,128)(2,1)} collective-permute-done((bf16[512,1024]{1,0:T(8,128)(2,1)}, bf16[512,1024]{1,0:T(8,128)(2,1)}, u32[]{:S(2)}, u32[]{:S(2)}) %collective-permute-start.4) | collective-permute-done | bytes 1048608 | tf_op jit(solution)/shard_map/ppermute | solution.py:223
  184.7 13.6 %fusion.112 = (bf16[2048]{0:T(1024)(128)(2,1)S(1)}, bf16[1024,2048]{1,0:T(8,128)(2,1)S(1)}) fusion(f32[1024,2048]{1,0:T(8,128)} %get-tuple-element.119, f32[2048]{0:T(1024)S(1)} %add.173, bf16[1024,4096]{1,0:T(8,128)(2,1)S(1)} %copy-done.28, bf16[512,1024]{1,0:T(8,128)(2,1)} %collective-permute-done.4, bf16[512,1024]{1,0:T(8,128)(2,1)} %param.31, ...), kind=kOutput, calls=%fused_computation.158 | convolution fusion | flops 4349491200 | bytes 18887680 | tf_op jit(solution)/shard_map/dot_general | solution.py:353
  202.3 22.2 %collective-permute-done.5 = bf16[512,1024]{1,0:T(8,128)(2,1)S(1)} collective-permute-done((bf16[512,1024]{1,0:T(8,128)(2,1)S(1)}, bf16[512,1024]{1,0:T(8,128)(2,1)S(1)}, u32[]{:S(2)}, u32[]{:S(2)}) %collective-permute-start.5) | collective-permute-done | bytes 1048608 | tf_op jit(solution)/shard_map/ppermute | solution.py:223
  224.4 3.1 multiply_reduce_fusion
  233.2 3.5 fusion.7
  241.5 12.7 %collective-permute-done.6 = bf16[512,1024]{1,0:T(8,128)(2,1)} collective-permute-done((bf16[512,1024]{1,0:T(8,128)(2,1)}, bf16[512,1024]{1,0:T(8,128)(2,1)}, u32[]{:S(2)}, u32[]{:S(2)}) %collective-permute-start.6) | collective-permute-done | bytes 1048608 | tf_op jit(solution)/shard_map/ppermute | solution.py:223
  254.2 3.9 convolution_convert_fusion.4.do_ref
  258.2 21.7 %attention_back.1 = (bf16[1024,512]{1,0:T(8,128)(2,1)S(1)}, bf16[1024,512]{1,0:T(8,128)(2,1)S(1)}, bf16[1024,512]{1,0:T(8,128)(2,1)S(1)}, f32[2,512]{1,0:T(2,128)S(1)}) custom-call(s32[1024,1]{1,0:T(8,128)S(1)} %copy-done.1, s32[1,1024]{1,0:T(1,128)S(1)} %bitcast.42, bf16[1024,1536]{1,0:T(8,128)(2,1)S(1)} %add_convert_fusion.q_ref.k_ref.v_ref, ...), custom_call_target="tpu_custom_call" | custom-call | flops 5368709120 | bytes 10485760 | tf_op jit(solution)/shard_map/attention_back/pallas_call | solution.py:195
  284.4 3.6 convolution_convert_fusion.3
  288.4 7.6 %convolution_convert_fusion = bf16[1024,1536]{1,0:T(8,128)(2,1)} fusion(bf16[1024,1536]{1,0:T(8,128)(2,1)} %copy-done.24, f32[1024]{0:T(1024)S(1)} %get-tuple-element.97, f32[1024]{0:T(1024)S(1)} %get-tuple-element.98, f32[1024]{0:T(1024)S(1)} %add_rsqrt_fusion, f32[1024]{0:T(1024)S(1)} %broadcast_multiply_fusion, bf16[512,1024]{1,0:T(8,128)(2,1)S(1)} %copy-done.10, ...), kind=kOutput, calls=%fused_computation.20 | convolution fusion | flops 3238526976 | bytes 8404993 | tf_op jit(solution)/shard_map/dot_general | solution.py:387
  296.0 9.1 %collective-permute-done.7 = bf16[512,1024]{1,0:T(8,128)(2,1)} collective-permute-done((bf16[512,1024]{1,0:T(8,128)(2,1)}, bf16[512,1024]{1,0:T(8,128)(2,1)}, u32[]{:S(2)}, u32[]{:S(2)}) %collective-permute-start.7) | collective-permute-done | bytes 1048608 | tf_op jit(solution)/shard_map/ppermute | solution.py:223
  305.1 6.1 %fusion.40 = (bf16[1024]{0:T(1024)(128)(2,1)S(1)}, bf16[1024]{0:T(1024)(128)(2,1)S(1)}, f32[512]{0:T(512)S(1)}, f32[512]{0:T(512)S(1)}, bf16[512,1024]{1,0:T(8,128)(2,1)}) fusion(bf16[512,1024]{1,0:T(8,128)(2,1)} %fusion.78, f32[1024,1024]{1,0:T(8,128)S(1)} %copy-done.19, s32[]{:T(128)S(6)} %select_n.50, s32[]{:T(128)S(6)} %select_n.54, ...), kind=kOutput, calls=%fused_computation.59 | convolution fusion | flops 1620046848 | bytes 13125120 | tf_op jit(solution)/shard_map/dot_general | solution.py:238
  313.0 3.3 concatenate.62
  316.4 3.6 fusion.9
  320.2 10.2 %convolution_convert_fusion.2 = bf16[1024,2048]{1,0:T(8,128)(2,1)} fusion(bf16[1024,2048]{1,0:T(8,128)(2,1)} %copy-done.31, bf16[512,1024]{1,0:T(8,128)(2,1)} %collective-permute-done.2, bf16[512,1024]{1,0:T(8,128)(2,1)} %add_convert_fusion.2, pred[]{:T(512)S(6)} %eq.22), kind=kOutput, calls=%fused_computation.22 | convolution fusion | flops 4306501632 | bytes 10485761 | tf_op jit(solution)/shard_map/dot_general | solution.py:357
  330.5 9.4 %convolution_convert_fusion.1 = bf16[1024,2048]{1,0:T(8,128)(2,1)} fusion(bf16[1024,2048]{1,0:T(8,128)(2,1)S(1)} %copy-done.29, bf16[512,1024]{1,0:T(8,128)(2,1)} %collective-permute-done.4, bf16[512,1024]{1,0:T(8,128)(2,1)} %param.31, pred[1024]{0:T(1024)(128)(4,1)S(1)} %get-tuple-element.110, pred[]{:T(512)S(6)} %eq.22), kind=kOutput, calls=%fused_computation.21 | convolution fusion | flops 4307550208 | bytes 10486785 | tf_op jit(solution)/shard_map/dot_general | solution.py:352
  339.9 7.8 %pad_maximum_fusion = bf16[1024,4096]{1,0:T(8,128)(2,1)} fusion(bf16[1024,2048]{1,0:T(8,128)(2,1)} %convolution_convert_fusion.1, bf16[1024,2048]{1,0:T(8,128)(2,1)} %convolution_convert_fusion.2), kind=kLoop, calls=%fused_computation.10 | loop fusion | flops 16777216 | bytes 16777216 | tf_op jit(solution)/shard_map/concatenate | solution.py:359
  347.7 5.5 %fusion.68 = bf16[512,1024]{1,0:T(8,128)(2,1)S(1)} fusion(bf16[1024,4096]{1,0:T(8,128)(2,1)} %all-gather.5.cloned.1.call-done, bf16[1024,2048]{1,0:T(8,128)(2,1)} %get-tuple-element.118, s32[]{:T(128)S(6)} %select_n.54), kind=kOutput, calls=%fused_computation.88 | convolution fusion | flops 2148007936 | bytes 7340036 | tf_op jit(solution)/shard_map/dot_general | solution.py:238
  355.0 19.4 %collective-permute-done.3 = bf16[512,1024]{1,0:T(8,128)(2,1)S(1)} collective-permute-done((bf16[512,1024]{1,0:T(8,128)(2,1)S(1)}, bf16[512,1024]{1,0:T(8,128)(2,1)S(1)}, u32[]{:S(2)}, u32[]{:S(2)}) %collective-permute-start.3) | collective-permute-done | bytes 1048608 | tf_op jit(solution)/shard_map/ppermute | solution.py:223
  374.7 6.2 %add_select_fusion = f32[512,1024]{1,0:T(8,128)} fusion(f32[512,1024]{1,0:T(8,128)S(1)} %copy-done.13, bf16[512,1024]{1,0:T(8,128)(2,1)S(1)} %collective-permute-done.3, f32[1024]{0:T(1024)S(1)} %get-tuple-element.92, pred[512]{0:T(512)(128)(4,1)S(1)} %dynamic_slice.33, bf16[1024,4096]{1,0:T(8,128)(2,1)} %all-gather.5.cloned.1.call-done, ...), kind=kOutput, calls=%fused_computation.73 | convolution fusion | flops 2151153664 | bytes 11538948 | tf_op jit(solution)/shard_map/dot_general | solution.py:238
  380.9 3.4 fusion.34
  384.3 8.3 %reduce-scatter.3.cloned.1.call-done = bf16[64,2176]{1,0:T(8,128)(2,1)} async-done(((bf16[1024,2176]{1,0:T(8,128)(2,1)}), bf16[64,2176]{1,0:T(8,128)(2,1)}) %reduce-scatter.3.cloned.1.call-update) | async-done | bytes 278544 | tf_op jit(solution)/shard_map/reduce_scatter | solution.py:263
  400.8 99.9 %reduce-scatter.5.cloned.1.call-done = bf16[64,4096]{1,0:T(8,128)(2,1)} async-done(((bf16[1024,4096]{1,0:T(8,128)(2,1)}), bf16[64,4096]{1,0:T(8,128)(2,1)}) %reduce-scatter.5.cloned.1.call-update) | async-done | bytes 524304 | tf_op jit(solution)/shard_map/reduce_scatter | solution.py:263
  (174 shorter events, 70.9 us)
Async XLA Ops:
  7.2 37.5 %copy-start.8 = (bf16[512,1024]{1,0:T(8,128)(2,1)S(1)}, bf16[512,1024]{1,0:T(8,128)(2,1)}, u32[]{:S(2)}) copy-start(bf16[512,1024]{1,0:T(8,128)(2,1)} %param.16) | copy-start | bytes 3145732
  7.2 15.8 %copy-start.26 = (s32[1024]{0:T(1024)S(1)}, s32[1024]{0:T(1024)}, u32[]{:S(2)}) copy-start(s32[1024]{0:T(1024)} %param.17) | copy-start | bytes 12292
  7.2 16.1 %copy-start.27 = (s32[8]{0:T(128)S(1)}, s32[8]{0:T(128)}, u32[]{:S(2)}) copy-start(s32[8]{0:T(128)} %param.18) | copy-start | bytes 100
  7.2 63.9 %all-gather.3.cloned.1.call-start = ((), (), s32[]{:S(2)}) async-start(), calls=%async_computation.2 | async-start | bytes 4734976 | tf_op jit(solution)/shard_map/all_gather | solution.py:303
  16.3 147.4 %all-gather.5.cloned.1.call-start = ((), (), s32[]{:S(2)}) async-start(), calls=%async_computation.3 | async-start | bytes 8912896 | tf_op jit(solution)/shard_map/all_gather | solution.py:304
  18.2 374.3 %reduce-scatter.3.cloned.1.call-start = ((), (), s32[]{:S(2)}) async-start(), calls=%async_computation.4 | async-start | bytes 4734976 | tf_op jit(solution)/shard_map/reduce_scatter | solution.py:263
  18.3 26.4 %collective-permute-start = (bf16[512,1024]{1,0:T(8,128)(2,1)}, bf16[512,1024]{1,0:T(8,128)(2,1)S(1)}, u32[]{:S(2)}, u32[]{:S(2)}) collective-permute-start(bf16[512,1024]{1,0:T(8,128)(2,1)} %param.16), channel_id=1, source_target_pairs={{0,1},{1,0},{2,3},{3,2},{4,5},{5,4},{6,7},{7,6},{8,9},{9,8},{10,11... | collective-permute-start | bytes 3145736 | tf_op jit(solution)/shard_map/ppermute | solution.py:223
  44.7 30.1 %copy-start.16 = (bf16[512,1024]{1,0:T(8,128)(2,1)}, bf16[512,1024]{1,0:T(8,128)(2,1)S(1)}, u32[]{:S(2)}) copy-start(bf16[512,1024]{1,0:T(8,128)(2,1)S(1)} %collective-permute-done) | copy-start | bytes 3145732
  105.7 25.6 %collective-permute-start.1 = (bf16[512,1024]{1,0:T(8,128)(2,1)}, bf16[512,1024]{1,0:T(8,128)(2,1)}, u32[]{:S(2)}, u32[]{:S(2)}) collective-permute-start(bf16[512,1024]{1,0:T(8,128)(2,1)} %convolution_convert_fusion.5), channel_id=1, source_target_pairs={{0,1},{1,0},{2,3},{3,2},{4,5},{5,4},{6,7},{7,6},{8,9},{9,8},{10,11... | collective-permute-start | bytes 3145736 | tf_op jit(solution)/shard_map/ppermute | solution.py:223
  137.3 26.4 %collective-permute-start.2 = (bf16[512,1024]{1,0:T(8,128)(2,1)}, bf16[512,1024]{1,0:T(8,128)(2,1)}, u32[]{:S(2)}, u32[]{:S(2)}) collective-permute-start(bf16[512,1024]{1,0:T(8,128)(2,1)} %add_convert_fusion.2), channel_id=1, source_target_pairs={{0,1},{1,0},{2,3},{3,2},{4,5},{5,4},{6,7},{7,6},{8,9},{9,8},{10,11... | collective-permute-start | bytes 3145736 | tf_op jit(solution)/shard_map/ppermute | solution.py:223
  138.7 45.9 %collective-permute-start.4 = (bf16[512,1024]{1,0:T(8,128)(2,1)}, bf16[512,1024]{1,0:T(8,128)(2,1)}, u32[]{:S(2)}, u32[]{:S(2)}) collective-permute-start(bf16[512,1024]{1,0:T(8,128)(2,1)} %param.31), channel_id=1, source_target_pairs={{0,1},{1,0},{2,3},{3,2},{4,5},{5,4},{6,7},{7,6},{8,9},{9,8},{10,11... | collective-permute-start | bytes 3145736 | tf_op jit(solution)/shard_map/ppermute | solution.py:223
  163.7 21.0 %copy-start.28 = (bf16[1024,4096]{1,0:T(8,128)(2,1)S(1)}, bf16[1024,4096]{1,0:T(8,128)(2,1)}, u32[]{:S(2)}) copy-start(bf16[1024,4096]{1,0:T(8,128)(2,1)} %all-gather.5.cloned.1.call-done) | copy-start | bytes 25165828
  198.2 26.2 %copy-start.31 = (bf16[1024,2048]{1,0:T(8,128)(2,1)}, bf16[1024,2048]{1,0:T(8,128)(2,1)S(1)}, u32[]{:S(2)}) copy-start(bf16[1024,2048]{1,0:T(8,128)(2,1)S(1)} %get-tuple-element.112) | copy-start | bytes 12582916
  198.3 26.2 %copy-start.12 = (f32[512,1024]{1,0:T(8,128)S(1)}, f32[512,1024]{1,0:T(8,128)}, u32[]{:S(2)}) copy-start(f32[512,1024]{1,0:T(8,128)} %copy-done.11) | copy-start | bytes 6291460
  200.7 23.8 %collective-permute-start.5 = (bf16[512,1024]{1,0:T(8,128)(2,1)S(1)}, bf16[512,1024]{1,0:T(8,128)(2,1)S(1)}, u32[]{:S(2)}, u32[]{:S(2)}) collective-permute-start(bf16[512,1024]{1,0:T(8,128)(2,1)S(1)} %fusion.58), channel_id=1, source_target_pairs={{0,1},{1,0},{2,3},{3,2},{4,5},{5,4},{6,7},{7,6},{8,9},{9,8},{10,11... | collective-permute-start | bytes 3145736 | tf_op jit(solution)/shard_map/ppermute | solution.py:223
  231.1 23.1 %collective-permute-start.6 = (bf16[512,1024]{1,0:T(8,128)(2,1)}, bf16[512,1024]{1,0:T(8,128)(2,1)}, u32[]{:S(2)}, u32[]{:S(2)}) collective-permute-start(bf16[512,1024]{1,0:T(8,128)(2,1)} %convert_element_type.133), channel_id=1, source_target_pairs={{0,1},{1,0},{2,3},{3,2},{4,5},{5,4},{6,7},{7,6},{8,9},{9,8},{10,11... | collective-permute-start | bytes 3145736 | tf_op jit(solution)/shard_map/ppermute | solution.py:223
  241.5 16.6 %copy-start.1 = (s32[1024,1]{1,0:T(8,128)S(1)}, s32[1024,1]{1,0:T(8,128)}, u32[]{:S(2)}) copy-start(s32[1024,1]{1,0:T(8,128)} %copy.102.seq_col_ref) | copy-start | bytes 12292
  241.5 16.6 %copy-start.3 = (f32[4,1024,2]{2,1,0:T(8,128)S(1)}, f32[4,1024,2]{2,1,0:T(8,128)}, u32[]{:S(2)}) copy-start(f32[4,1024,2]{2,1,0:T(8,128)} %copy-done.2) | copy-start | bytes 98308
  241.5 16.6 %copy-start.5 = (bf16[1024,512]{1,0:T(8,128)(2,1)S(1)}, bf16[1024,512]{1,0:T(8,128)(2,1)}, u32[]{:S(2)}) copy-start(bf16[1024,512]{1,0:T(8,128)(2,1)} %copy-done.4) | copy-start | bytes 3145732
  254.2 25.9 %slice-start = ((s8[4456448]{0:T(1024)(128)(4,1)}), s8[4194304]{0:T(1024)(128)(4,1)S(1)}, s32[]{:S(2)}) async-start(s8[4456448]{0:T(1024)(128)(4,1)} %bitcast.54), calls=%async_computation.6 | async-start | bytes 8388608
  258.2 22.0 %slice-start.1 = ((s8[4456448]{0:T(1024)(128)(4,1)}), s8[262144]{0:T(1024)(128)(4,1)S(1)}, s32[]{:S(2)}) async-start(s8[4456448]{0:T(1024)(128)(4,1)} %bitcast.54), calls=%async_computation.7 | async-start | bytes 524288
  283.0 22.2 %collective-permute-start.7 = (bf16[512,1024]{1,0:T(8,128)(2,1)}, bf16[512,1024]{1,0:T(8,128)(2,1)}, u32[]{:S(2)}, u32[]{:S(2)}) collective-permute-start(bf16[512,1024]{1,0:T(8,128)(2,1)} %fusion.78), channel_id=1, source_target_pairs={{0,1},{1,0},{2,3},{3,2},{4,5},{5,4},{6,7},{7,6},{8,9},{9,8},{10,11... | collective-permute-start | bytes 3145736 | tf_op jit(solution)/shard_map/ppermute | solution.py:223
  288.4 16.7 %copy-start.19 = (f32[1024,1024]{1,0:T(8,128)S(1)}, f32[1024,1024]{1,0:T(8,128)}, u32[]{:S(2)}) copy-start(f32[1024,1024]{1,0:T(8,128)} %fusion.7) | copy-start | bytes 12582916
  288.4 16.7 %copy-start.25 = (bf16[1024,1536]{1,0:T(8,128)(2,1)S(1)}, bf16[1024,1536]{1,0:T(8,128)(2,1)}, u32[]{:S(2)}) copy-start(bf16[1024,1536]{1,0:T(8,128)(2,1)} %copy-done.24) | copy-start | bytes 9437188
  296.0 17.0 %copy-start.20 = (bf16[1024,2]{1,0:T(8,128)(2,1)S(1)}, bf16[1024,2]{1,0:T(8,128)(2,1)}, u32[]{:S(2)}) copy-start(bf16[1024,2]{1,0:T(8,128)(2,1)} %reshape.175) | copy-start | bytes 12292
  296.0 17.0 %copy-start.21 = (bf16[1024,1]{1,0:T(8,128)(2,1)S(1)}, bf16[1024,1]{1,0:T(8,128)(2,1)}, u32[]{:S(2)}) copy-start(bf16[1024,1]{1,0:T(8,128)(2,1)} %stack.56) | copy-start | bytes 6148
  296.0 17.0 %copy-start.22 = (bf16[1024,1]{1,0:T(8,128)(2,1)S(1)}, bf16[1024,1]{1,0:T(8,128)(2,1)}, u32[]{:S(2)}) copy-start(bf16[1024,1]{1,0:T(8,128)(2,1)} %stack.57) | copy-start | bytes 6148
  320.0 180.7 %reduce-scatter.5.cloned.1.call-start = ((), (), s32[]{:S(2)}) async-start(), calls=%async_computation.5 | async-start | bytes 8912896 | tf_op jit(solution)/shard_map/reduce_scatter | solution.py:263
  347.7 26.9 %copy-start.13 = (f32[512,1024]{1,0:T(8,128)S(1)}, f32[512,1024]{1,0:T(8,128)}, u32[]{:S(2)}) copy-start(f32[512,1024]{1,0:T(8,128)} %copy-done.11) | copy-start | bytes 6291460
  347.7 26.9 %copy-start.30 = (bf16[1024,2048]{1,0:T(8,128)(2,1)S(1)}, bf16[1024,2048]{1,0:T(8,128)(2,1)}, u32[]{:S(2)}) copy-start(bf16[1024,2048]{1,0:T(8,128)(2,1)} %get-tuple-element.118) | copy-start | bytes 12582916
  353.2 21.2 %collective-permute-start.3 = (bf16[512,1024]{1,0:T(8,128)(2,1)S(1)}, bf16[512,1024]{1,0:T(8,128)(2,1)S(1)}, u32[]{:S(2)}, u32[]{:S(2)}) collective-permute-start(bf16[512,1024]{1,0:T(8,128)(2,1)S(1)} %fusion.68), channel_id=1, source_target_pairs={{0,1},{1,0},{2,3},{3,2},{4,5},{5,4},{6,7},{7,6},{8,9},{9,8},{10,11... | collective-permute-start | bytes 3145736 | tf_op jit(solution)/shard_map/ppermute | solution.py:223
  393.6 6.4 %collective-permute-start.8 = (f32[6,64]{0,1:T(8,128)S(1)}, f32[6,64]{0,1:T(8,128)S(1)}, u32[]{:S(2)}, u32[]{:S(2)}) collective-permute-start(f32[6,64]{0,1:T(8,128)S(1)} %slice_bitcast_fusion.2), channel_id=1, source_target_pairs={{0,1},{1,0},{2,3},{3,2},{4,5},{5,4},{6,7},{7,6},{8,9},{9,8},{10,11... | collective-permute-start | bytes 4616 | tf_op jit(solution)/shard_map/ppermute | solution.py:223
  (15 other events, 65.2 us)
Sparse Core Ops, SparseCore 0:
  16.4 54.6 all-gather.2
  73.9 73.3 all-gather.4
  320.1 72.4 reduce-scatter.2
  397.0 103.6 reduce-scatter.4

commit v2 on v1

--- a/solution.py
+++ b/solution.py
@@ -249,6 +249,21 @@
     return keep.astype(f32) + arrived.astype(f32), (send, keep)
 
 
+def row_blocks(block):
+    if lax.axis_size("tensor") != 2:
+        return [lax.all_gather(block, "tensor", axis=0, tiled=True)]
+    return [block, swap(block)]
+
+
+def block_sum(blocks, right):
+    product = lambda rows: lax.dot_general(rows, right, NT, preferred_element_type=f32).astype(bf16)
+    if len(blocks) == 1:
+        total = lax.psum_scatter(product(blocks[0]), "tensor", scatter_dimension=0, tiled=True)
+        return total, jnp.zeros_like(total)
+    arrived = swap(product(blocks[1]))
+    return product(blocks[0]), arrived
+
+
 def as_columns(vector, rows):
     flat = vector.reshape(-1)
     columns = -(-flat.shape[0] // rows)
@@ -261,6 +276,24 @@
 
 def scatter_groups(array):
     return lax.psum_scatter(array, "dp", scatter_dimension=0, tiled=True).astype(f32)
+
+
+def halving_sum(array):
+    devices = lax.axis_size("dp")
+    if devices & (devices - 1):
+        return scatter_groups(array)
+    place = lax.axis_index("dp")
+    rows, columns = array.shape[0] // devices, array.shape[1]
+    step = 1
+    while step < devices:
+        halves = array.reshape(devices // (2 * step), 2, rows, columns)
+        bit = (place // step) % 2
+        half = lambda which: lax.dynamic_index_in_dim(halves, which, 1, keepdims=False)
+        arrived = lax.ppermute(half(1 - bit), "dp", [(i, i ^ step) for i in range(devices)])
+        total = half(bit).astype(f32) + arrived.astype(f32)
+        step *= 2
+        array = total.astype(bf16)
+    return total.reshape(rows, columns)
 
 
 def local(
@@ -335,8 +368,19 @@
     key_row = jnp.where(live, slot_seq, -1)[None, :]
 
     tokens_all = gather_rows(tokens)
-    cotangent_all = gather_rows(cotangent)
-    grad_h2_all = jnp.where(live[:, None], cotangent_all, jnp.zeros_like(cotangent_all))
+    tokens_all, cotangent = lax.optimization_barrier((tokens_all, cotangent))
+    live_blocks = [live]
+    if lax.axis_size("tensor") == 2:
+        live_blocks = [
+            own_live,
+            lax.dynamic_slice_in_dim(live, (1 - me) * own_rows, own_rows),
+        ]
+    grad_h2_blocks = [
+        jnp.where(here_live[:, None], block, jnp.zeros_like(block))
+        for here_live, block in zip(live_blocks, row_blocks(cotangent))
+    ]
+    tokens_all, grad_h2_blocks = lax.optimization_barrier((tokens_all, grad_h2_blocks))
+    grad_h2_all = jnp.concatenate(grad_h2_blocks, axis=0)
 
     a1_full, normed_one_all, _ = layer_norm(tokens_all.astype(f32), gain_one, shift_one)
     a1_all = a1_full.astype(bf16)
@@ -346,21 +390,35 @@
     inputs = tokens.astype(f32)
     hidden_one = inputs + attn + bias_out
     a2_full, normed_two, inverse_two = layer_norm(hidden_one, gain_two, shift_two)
-    a2_all = gather_rows(a2_full.astype(bf16))
-    pre = jnp.dot(a2_all, w_up, preferred_element_type=f32) + bias_up
-    act = gelu_value(pre).astype(bf16)
+    a2_blocks = row_blocks(a2_full.astype(bf16))
+    act_blocks, grad_pre_blocks = [], []
+    grad_up_bias = 0.0
+    for index, (a2_block, grad_block) in enumerate(zip(a2_blocks, grad_h2_blocks)):
+        pre = jnp.dot(a2_block, w_up, preferred_element_type=f32) + bias_up
+        act_blocks.append(gelu_value(pre).astype(bf16))
+        grad_pre = jnp.dot(grad_block, w_down_t, preferred_element_type=f32) * gelu_slope(pre)
+        grad_up_bias = grad_up_bias + jnp.sum(grad_pre, axis=0)
+        grad_pre_blocks.append(grad_pre.astype(bf16))
+        if index + 1 < len(a2_blocks):
+            act_blocks[0], grad_pre_blocks[0], grad_up_bias, a2_blocks[1] = (
+                lax.optimization_barrier(
+                    (act_blocks[0], grad_pre_blocks[0], grad_up_bias, a2_blocks[1])
+                )
+            )
+    act = jnp.concatenate(act_blocks, axis=0)
+    grad_pre_b = jnp.concatenate(grad_pre_blocks, axis=0)
+    a2_all = jnp.concatenate(a2_blocks, axis=0)
+    grad_a2_keep, grad_a2_arrived = block_sum(grad_pre_blocks, w_up)
     grad_down_weight_t = lax.dot_general(grad_h2_all, act, TN, preferred_element_type=f32)
-    grad_pre = jnp.dot(grad_h2_all, w_down_t, preferred_element_type=f32) * gelu_slope(pre)
-    grad_up_bias = jnp.sum(grad_pre, axis=0)
-    grad_pre_b = grad_pre.astype(bf16)
-    grad_a2, _ = own_sum(grad_pre_b, w_up, own_rows)
     grad_up_weight = lax.dot_general(a2_all, grad_pre_b, TN, preferred_element_type=f32)
-    second_sum = scatter_groups(
-        jnp.concatenate([grad_up_weight.astype(bf16), grad_down_weight_t.astype(bf16)], axis=1)
-    )
-
-    mlp, _ = own_sum(act, w_down_t, own_rows)
-    output = jnp.where(own_live[:, None], hidden_one + mlp + bias_down, 0.0)
+    second_piece = jnp.concatenate(
+        [grad_up_weight.astype(bf16), grad_down_weight_t.astype(bf16)], axis=1
+    )
+    grad_a2_keep, grad_a2_arrived, second_piece = lax.optimization_barrier(
+        (grad_a2_keep, grad_a2_arrived, second_piece)
+    )
+    second_sum = scatter_groups(second_piece)
+    grad_a2 = grad_a2_keep.astype(f32) + grad_a2_arrived.astype(f32)
 
     grad_h2 = jnp.where(own_live[:, None], cotangent.astype(f32), 0.0)
     grad_down_bias = jnp.sum(grad_h2, axis=0)
@@ -369,11 +427,18 @@
     grad_h1 = grad_h2 + norm_back(grad_a2, gain_two, normed_two, inverse_two)
     grad_out_bias = jnp.sum(grad_h1, axis=0)
     grad_h1_all = gather_rows(grad_h1.astype(bf16))
+    grad_h1_all, act_blocks = lax.optimization_barrier((grad_h1_all, act_blocks))
+    mlp_keep, mlp_arrived = block_sum(act_blocks, w_down_t)
     grad_heads = jnp.dot(grad_h1_all, w_out_t, preferred_element_type=f32).astype(bf16)
     grad_out_weight_t = lax.dot_general(grad_h1_all, heads, TN, preferred_element_type=f32)
     dq, dk, dv, grad_qkv_bias = attention_back(
         qkv, seq_col, key_row, heads, lse, grad_heads, pairs
     )
+    dq, dk, dv, mlp_keep, mlp_arrived = lax.optimization_barrier(
+        (dq, dk, dv, mlp_keep, mlp_arrived)
+    )
+    mlp = mlp_keep.astype(f32) + mlp_arrived.astype(f32)
+    output = jnp.where(own_live[:, None], hidden_one + mlp + bias_down, 0.0)
     grad_qkv = jnp.concatenate([dq, dk, dv], axis=1)
     grad_a1, parts = own_sum(grad_qkv, w_qkv, own_rows)
     if lax.axis_size("tensor") == 2:
@@ -414,20 +479,12 @@
             axis=1,
         )
     )
-    first_sum = scatter_groups(
-        jnp.concatenate(
-            [
-                grad_qkv_weight.astype(bf16),
-                grad_out_weight_t.astype(bf16),
-                grad_small.astype(bf16),
-            ],
-            axis=1,
-        )
-    )
+    out_sum = halving_sum(grad_out_weight_t.astype(bf16))
+    qkv_sum = halving_sum(grad_qkv_weight.astype(bf16))
+    small_sum = halving_sum(grad_small.astype(bf16))
     normed_one, inverse_one = layer_norm(inputs, gain_one, shift_one)[1:]
     grad_tokens = grad_h1 + norm_back(grad_a1, gain_one, normed_one, inverse_one)
 
-    small_sum = first_sum[:, 4 * here :]
     vector_sum = small_sum[:, :6].T
     if lax.axis_size("tensor") == 2:
         vector_sum = vector_sum + swap(vector_sum)
@@ -441,9 +498,9 @@
         grad_tokens,
         vector_sum[0],
         vector_sum[1],
-        first_sum[:, : 3 * here].reshape(shard, 3, here),
+        qkv_sum.reshape(shard, 3, here),
         qkv_bias_sum[: qkv_bias.size].reshape(qkv_bias.shape),
-        first_sum[:, 3 * here : 4 * here].T,
+        out_sum.T,
         vector_sum[2],
         vector_sum[3],
         vector_sum[4],

time: 520 us -> 393 us (0.76)
  waiting for transfers between devices: 269 us -> 129 us
  matrix products: 99.9 us -> 79.7 us
  other arithmetic: 34.4 us -> 51 us
  local copies, waits for them, and re-layouts: 38.4 us -> 48.3 us
  starting transfers between devices: 14.6 us -> 23.4 us
    reduce_scatter x2 -> x1, waiting for transfers between devices: 108 us -> 0.01 us  [scatter_groups(): lax.psum_scatter(array, 'dp', scatter_dimension=0, tiled=True).astype(f32)]
    ppermute x9, waiting for transfers between devices: 138 us -> 80.6 us  [swap(): return lax.ppermute(block, 'tensor', [(0, 1), (1, 0)])]
    ppermute x0 -> x12, waiting for transfers between devices: none -> 39.9 us  [halving_sum(): lax.ppermute(half(1 - bit), 'dp', [(i, i ^ step) for i in range(devices)])]
    all_gather x1, waiting for transfers between devices: 23.3 us -> 0.02 us  [local(): first_all = lax.all_gather(first_piece, 'dp', axis=0, tiled=True)]
    dot_general x8 -> x4, matrix products: 32.1 us -> 14 us  [own_sum(): lax.dot_general(rows, right, NT, preferred_element_type=f32).astype(bf16)]
    select_n x0 -> x5, other arithmetic: none -> 13 us  [the longest x2 6.29 us: gather_rows(): jnp.where(lax.axis_index('tensor') == 0, jnp.concatenate([block, other],...]
    dot_general x2 -> x8, matrix products: 25.9 us -> 36.5 us  [the longest x4 16.5 us: block_sum(): lax.dot_general(rows, right, NT, preferred_element_type=f32).astype(bf16)]
    unnamed x74 -> x111, local copies, waits for them, and re-layouts: 7.19 us -> 16.5 us
  transfers between devices with their start and end apart: 13 -> 24, of which waited for: 11 -> 15; matrix products, arithmetic and copies ran while one was open for 22% -> 35% of each run, Pallas kernels for 4% -> 10%
where the time goes in v2:
time: 393 us; the launch traced here: 386 us
  waiting for transfers between devices  129 us (33%)
  matrix products  79.7 us (20%)
  other arithmetic  51 us (13%)
  local copies, waits for them, and re-layouts  48.3 us (12%)
  Pallas kernels  39.8 us (10%)
  starting transfers between devices  23.4 us (6%)
  between operations  15.2 us (4%)
    ppermute x9, waiting for transfers between devices, swap(): return lax.ppermute(block, 'tensor', [(0, 1), (1, 0)])  80.6 us
    ppermute x12, waiting for transfers between devices, halving_sum(): lax.ppermute(half(1 - bit), 'dp', [(i, i ^ step) for i in range(devices)])  39.9 us
    pallas_call x1, Pallas kernels, attention_back(): pl.pallas_call(functools.partial(attention_back_kernel, rows), grid=(pair...  21.5 us
    pallas_call x1, Pallas kernels, attention(): pl.pallas_call(functools.partial(attention_kernel, rows), grid=(pairs,),...  18.3 us
    unnamed x111, local copies, waits for them, and re-layouts  16.5 us
    dot_general x4, matrix products, block_sum(): lax.dot_general(rows, right, NT, preferred_element_type=f32).astype(bf16)  16.5 us
    ppermute x9, starting transfers between devices, swap(): return lax.ppermute(block, 'tensor', [(0, 1), (1, 0)])  15.3 us
    dot_general x4, matrix products, own_sum(): lax.dot_general(rows, right, NT, preferred_element_type=f32).astype(bf16)  14 us
  transfers between devices with their start and end apart: 24, of which 15 were waited for; matrix products, arithmetic and copies ran while one was open for 35% of the time, Pallas kernels for 10%

profile of v2, /device:TPU:0, one launch (start us, length us, event | category | flops | bytes accessed | tf_op | source)
XLA Modules:
  0.0 386.0 jit_solution(14175102215613688905)
XLA Ops:
  22.3 22.4 %collective-permute-done = bf16[512,1024]{1,0:T(8,128)(2,1)} collective-permute-done((bf16[512,1024]{1,0:T(8,128)(2,1)}, bf16[512,1024]{1,0:T(8,128)(2,1)}, u32[]{:S(2)}, u32[]{:S(2)}) %collective-permute-start) | collective-permute-done | bytes 1048608 | tf_op jit(solution)/shard_map/ppermute | solution.py:223
  52.1 19.9 %collective-permute-done.1 = bf16[512,1024]{1,0:T(8,128)(2,1)S(1)} collective-permute-done((bf16[512,1024]{1,0:T(8,128)(2,1)}, bf16[512,1024]{1,0:T(8,128)(2,1)S(1)}, u32[]{:S(2)}, u32[]{:S(2)}) %collective-permute-start.1) | collective-permute-done | bytes 1048608 | tf_op jit(solution)/shard_map/ppermute | solution.py:223
  78.3 6.5 %add_convert_fusion.q_ref.k_ref.v_ref = bf16[1024,1536]{1,0:T(8,128)(2,1)S(1)} fusion(f32[1536]{0:T(1024)S(1)} %pad_maximum_fusion.2, bf16[1024,2176]{1,0:T(8,128)(2,1)} %all-gather.3.cloned.1.call-done, f32[1024]{0:T(1024)S(1)} %get-tuple-element.179, f32[1024]{0:T(1024)S(1)} %get-tuple-element.180, bf16[1024,1024]{1,0:T(8,128)(2,1)} %copy-done.16, ...), kind=kOutput, calls=%fused_computation.5 | convolution fusion | flops 3230662656 | bytes 8411136 | tf_op jit(solution)/shard_map/dot_general | solution.py:387
  84.8 18.3 %attention.1 = (bf16[1024,512]{1,0:T(8,128)(2,1)S(1)}, f32[4,1024,2]{2,1,0:T(8,128)S(1)}) custom-call(s32[1024,1]{1,0:T(8,128)S(1)} %copy-done, s32[1,1024]{1,0:T(1,128)S(1)} %bitcast.107, bf16[1024,1536]{1,0:T(8,128)(2,1)S(1)} %add_convert_fusion.q_ref.k_ref.v_ref, bf16[1024,1536]{1,0:T(8,128)(2,1)S(1)} %add_convert_fusion.q_ref.k_ref.v_ref, ...), custom_call_target="tpu_custom_call" | custom-call | flops 2147483648 | bytes 6291456 | tf_op jit(solution)/shard_map/attention/pallas_call | solution.py:109
  105.5 3.5 convolution_convert_fusion.3
  114.7 17.1 %collective-permute-done.2 = bf16[512,1024]{1,0:T(8,128)(2,1)} collective-permute-done((bf16[512,1024]{1,0:T(8,128)(2,1)}, bf16[512,1024]{1,0:T(8,128)(2,1)}, u32[]{:S(2)}, u32[]{:S(2)}) %collective-permute-start.2) | collective-permute-done | bytes 1048608 | tf_op jit(solution)/shard_map/ppermute | solution.py:223
  138.7 8.0 %all-gather.5.cloned.1.call-done = bf16[1024,4096]{1,0:T(8,128)(2,1)} async-done(((bf16[64,4096]{1,0:T(8,128)(2,1)}), bf16[1024,4096]{1,0:T(8,128)(2,1)}) %all-gather.5.cloned.1.call-update) | async-done | bytes 8388624 | tf_op jit(solution)/shard_map/all_gather | solution.py:337
  146.7 5.5 %multiply_convert_fusion.1 = (bf16[512,2048]{1,0:T(8,128)(2,1)S(1)}, f32[512,2048]{1,0:T(8,128)S(1)}) fusion(f32[2048]{0:T(1024)S(1)} %add.308, bf16[512,1024]{1,0:T(8,128)(2,1)} %add_convert_fusion.2, bf16[1024,4096]{1,0:T(8,128)(2,1)} %all-gather.5.cloned.1.call-done), kind=kOutput, calls=%fused_computation.32 | convolution fusion | flops 2157969408 | bytes 11542528 | tf_op jit(solution)/shard_map/dot_general | solution.py:397
  152.2 5.2 %fusion.124 = (f32[2048]{0:T(1024)S(1)}, bf16[512,2048]{1,0:T(8,128)(2,1)S(1)}) fusion(f32[512,2048]{1,0:T(8,128)S(1)} %get-tuple-element.205, f32[2048]{0:T(1024)S(1)} %add.308, bf16[512,1024]{1,0:T(8,128)(2,1)S(1)} %copy-done.27, bf16[1024,4096]{1,0:T(8,128)(2,1)S(1)} %copy-done.43), kind=kOutput, calls=%fused_computation.203 | convolution fusion | flops 2169501696 | bytes 11550720 | tf_op jit(solution)/shard_map/dot_general | solution.py:399
  159.4 4.6 %multiply_convert_fusion = (bf16[512,2048]{1,0:T(8,128)(2,1)S(1)}, f32[512,2048]{1,0:T(8,128)S(1)}) fusion(f32[2048]{0:T(1024)S(1)} %add.308, bf16[512,1024]{1,0:T(8,128)(2,1)} %collective-permute-done.3, bf16[1024,4096]{1,0:T(8,128)(2,1)S(1)} %copy-done.43), kind=kOutput, calls=%fused_computation.31 | convolution fusion | flops 2157969408 | bytes 11542528 | tf_op jit(solution)/shard_map/dot_general | solution.py:397
  164.1 4.7 %fusion.123 = (f32[2048]{0:T(1024)S(1)}, bf16[512,2048]{1,0:T(8,128)(2,1)S(1)}) fusion(f32[512,2048]{1,0:T(8,128)S(1)} %get-tuple-element.209, f32[2048]{0:T(1024)S(1)} %add.308, bf16[512,1024]{1,0:T(8,128)(2,1)S(1)} %copy-done.28, bf16[1024,4096]{1,0:T(8,128)(2,1)S(1)} %copy-done.43), kind=kOutput, calls=%fused_computation.202 | convolution fusion | flops 2169501696 | bytes 11550720 | tf_op jit(solution)/shard_map/dot_general | solution.py:399
  173.1 7.8 %fusion.26 = bf16[1024,2048]{1,0:T(8,128)(2,1)} fusion(bf16[512,2048]{1,0:T(8,128)(2,1)S(1)} %get-tuple-element.194, bf16[512,2048]{1,0:T(8,128)(2,1)S(1)} %get-tuple-element.46, bf16[512,1024]{1,0:T(8,128)(2,1)} %collective-permute-done.3, bf16[512,1024]{1,0:T(8,128)(2,1)} %add_convert_fusion.2), kind=kOutput, calls=%fused_computation.35 | convolution fusion | flops 4309647360 | bytes 10485760 | tf_op jit(solution)/shard_map/dot_general | solution.py:413
  180.9 6.4 %fusion.23 = bf16[1024,2048]{1,0:T(8,128)(2,1)} fusion(bf16[512,2048]{1,0:T(8,128)(2,1)S(1)} %get-tuple-element.57, bf16[512,2048]{1,0:T(8,128)(2,1)S(1)} %get-tuple-element.56, bf16[512,1024]{1,0:T(8,128)(2,1)S(1)} %copy-done.28, bf16[512,1024]{1,0:T(8,128)(2,1)S(1)} %copy-done.27), kind=kOutput, calls=%fused_computation.34 | convolution fusion | flops 4309647360 | bytes 10485760 | tf_op jit(solution)/shard_map/dot_general | solution.py:412
  190.6 7.8 %pad_maximum_fusion = bf16[1024,4096]{1,0:T(8,128)(2,1)} fusion(bf16[1024,2048]{1,0:T(8,128)(2,1)} %fusion.23, bf16[1024,2048]{1,0:T(8,128)(2,1)} %fusion.26), kind=kLoop, calls=%fused_computation | loop fusion | flops 16777216 | bytes 16777216 | tf_op jit(solution)/shard_map/concatenate | solution.py:414
  198.4 4.0 %multiply_reduce_fusion = (bf16[1024]{0:T(1024)(128)(2,1)}, f32[512]{0:T(512)S(1)}, f32[512]{0:T(512)S(1)}, bf16[1024]{0:T(1024)(128)(2,1)}) fusion(bf16[512,1024]{1,0:T(8,128)(2,1)} %collective-permute-done.4, bf16[512,1024]{1,0:T(8,128)(2,1)} %fusion.87, f32[512,1024]{1,0:T(8,128)} %copy-done.11, f32[512]{0:T(512)S(1)} %add_rsqrt_fusion.2, ...), kind=kLoop, calls=%fused_computation.87 | loop fusion | flops 6288384 | bytes 4210688 | tf_op jit(solution)/shard_map/reduce_sum | solution.py:425
  211.3 4.0 %fusion = f32[1024,1024]{1,0:T(8,128)} fusion(bf16[1024,1024]{1,0:T(8,128)(2,1)} %copy-done.16, f32[1024]{0:T(1024)S(1)} %add_rsqrt_fusion, f32[1024]{0:T(1024)S(1)} %broadcast_multiply_fusion), kind=kLoop, calls=%fused_computation.8 | loop fusion | flops 3145728 | bytes 6299648 | tf_op jit(solution)/shard_map/mul | solution.py:22
  222.2 9.7 %collective-permute-done.5 = bf16[512,1024]{1,0:T(8,128)(2,1)} collective-permute-done((bf16[512,1024]{1,0:T(8,128)(2,1)}, bf16[512,1024]{1,0:T(8,128)(2,1)}, u32[]{:S(2)}, u32[]{:S(2)}) %collective-permute-start.5) | collective-permute-done | bytes 1048608 | tf_op jit(solution)/shard_map/ppermute | solution.py:223
  231.9 3.7 maximum_select_fusion.1
  237.3 6.4 %fusion.96 = bf16[512,1024]{1,0:T(8,128)(2,1)} fusion(bf16[512,2048]{1,0:T(8,128)(2,1)S(1)} %copy-done.47, bf16[1024,4096]{1,0:T(8,128)(2,1)} %all-gather.5.cloned.1.call-done), kind=kOutput, calls=%fused_computation.115 | convolution fusion | flops 2148007936 | bytes 7340032 | tf_op jit(solution)/shard_map/dot_general | solution.py:259
  248.5 4.5 %collective-permute-done.18 = bf16[4,64,512]{2,1,0:T(8,128)(2,1)S(1)} collective-permute-done((bf16[4,64,512]{2,1,0:T(8,128)(2,1)S(1)}, bf16[4,64,512]{2,1,0:T(8,128)(2,1)S(1)}, u32[]{:S(2)}, u32[]{:S(2)}) %collective-permute-start.18) | collective-permute-done | bytes 262176 | tf_op jit(solution)/shard_map/ppermute | solution.py:292
  256.8 6.6 %collective-permute-done.19 = bf16[2,64,512]{2,1,0:T(8,128)(2,1)S(1)} collective-permute-done((bf16[2,64,512]{2,1,0:T(8,128)(2,1)S(1)}, bf16[2,64,512]{2,1,0:T(8,128)(2,1)S(1)}, u32[]{:S(2)}, u32[]{:S(2)}) %collective-permute-start.19) | collective-permute-done | bytes 131104 | tf_op jit(solution)/shard_map/ppermute | solution.py:292
  264.1 21.5 %attention_back.1 = (bf16[1024,512]{1,0:T(8,128)(2,1)S(1)}, bf16[1024,512]{1,0:T(8,128)(2,1)S(1)}, bf16[1024,512]{1,0:T(8,128)(2,1)S(1)}, f32[2,512]{1,0:T(2,128)S(1)}) custom-call(s32[1024,1]{1,0:T(8,128)S(1)} %copy-done.1, s32[1,1024]{1,0:T(1,128)S(1)} %bitcast.108, bf16[1024,1536]{1,0:T(8,128)(2,1)S(1)} %add_convert_fusion.q_ref.k_ref.v_ref, ...), custom_call_target="tpu_custom_call" | custom-call | flops 5368709120 | bytes 10485760 | tf_op jit(solution)/shard_map/attention_back/pallas_call | solution.py:195
  292.3 3.9 %fusion.82 = bf16[512,1024]{1,0:T(8,128)(2,1)S(1)} fusion(bf16[1024,2176]{1,0:T(8,128)(2,1)} %all-gather.3.cloned.1.call-done, bf16[1024,1536]{1,0:T(8,128)(2,1)S(1)} %constant_dynamic-update-slice_fusion, s32[]{:T(128)S(6)} %select_n.153), kind=kOutput, calls=%fused_computation.107 | convolution fusion | flops 1611137024 | bytes 5767172 | tf_op jit(solution)/shard_map/dot_general | solution.py:238
  296.1 3.6 collective-permute-start.7
  299.7 4.1 %convolution_convert_fusion = bf16[1024,1536]{1,0:T(8,128)(2,1)S(1)} fusion(bf16[1024,1536]{1,0:T(8,128)(2,1)S(1)} %constant_dynamic-update-slice_fusion, f32[1024]{0:T(1024)S(1)} %copy-done.41, f32[1024]{0:T(1024)S(1)} %copy-done.35, bf16[1024,1024]{1,0:T(8,128)(2,1)S(1)} %copy-done.17, f32[1024]{0:T(1024)S(1)} %add_rsqrt_fusion, ...), kind=kOutput, calls=%fused_computation.36 | convolution fusion | flops 3229089792 | bytes 8404992 | tf_op jit(solution)/shard_map/dot_general | solution.py:452
  310.6 9.3 %collective-permute-done.7 = bf16[512,1024]{1,0:T(8,128)(2,1)S(1)} collective-permute-done((bf16[512,1024]{1,0:T(8,128)(2,1)S(1)}, bf16[512,1024]{1,0:T(8,128)(2,1)S(1)}, u32[]{:S(2)}, u32[]{:S(2)}) %collective-permute-start.7) | collective-permute-done | bytes 1048608 | tf_op jit(solution)/shard_map/ppermute | solution.py:223
  320.0 3.7 fusion.62
  330.5 4.2 %collective-permute-done.9 = bf16[4,64,128]{2,1,0:T(8,128)(2,1)S(1)} collective-permute-done((bf16[4,64,128]{2,1,0:T(8,128)(2,1)S(1)}, bf16[4,64,128]{2,1,0:T(8,128)(2,1)S(1)}, u32[]{:S(2)}, u32[]{:S(2)}) %collective-permute-start.9) | collective-permute-done | bytes 65568 | tf_op jit(solution)/shard_map/ppermute | solution.py:292
  343.8 11.7 %collective-permute-done.14 = bf16[4,64,1536]{2,1,0:T(8,128)(2,1)S(1)} collective-permute-done((bf16[4,64,1536]{2,1,0:T(8,128)(2,1)S(1)}, bf16[4,64,1536]{2,1,0:T(8,128)(2,1)S(1)}, u32[]{:S(2)}, u32[]{:S(2)}) %collective-permute-start.14) | collective-permute-done | bytes 786464 | tf_op jit(solution)/shard_map/ppermute | solution.py:292
  359.4 5.5 %collective-permute-done.15 = bf16[2,64,1536]{2,1,0:T(8,128)(2,1)S(1)} collective-permute-done((bf16[2,64,1536]{2,1,0:T(8,128)(2,1)S(1)}, bf16[2,64,1536]{2,1,0:T(8,128)(2,1)S(1)}, u32[]{:S(2)}, u32[]{:S(2)}) %collective-permute-start.15) | collective-permute-done | bytes 393248 | tf_op jit(solution)/shard_map/ppermute | solution.py:292
  365.0 3.8 collective-permute-start.16
  369.6 4.6 %collective-permute-done.16 = bf16[1,64,1536]{2,1,0:T(8,128)(2,1)S(1)} collective-permute-done((bf16[1,64,1536]{2,1,0:T(8,128)(2,1)S(1)}, bf16[1,64,1536]{2,1,0:T(8,128)(2,1)S(1)}, u32[]{:S(2)}, u32[]{:S(2)}) %collective-permute-start.16) | collective-permute-done | bytes 196640 | tf_op jit(solution)/shard_map/ppermute | solution.py:292
  (263 shorter events, 118.4 us)
Async XLA Ops:
  7.2 37.6 %copy-start.20 = (bf16[512,1024]{1,0:T(8,128)(2,1)S(1)}, bf16[512,1024]{1,0:T(8,128)(2,1)}, u32[]{:S(2)}) copy-start(bf16[512,1024]{1,0:T(8,128)(2,1)} %param.16) | copy-start | bytes 3145732
  7.2 67.0 %all-gather.3.cloned.1.call-start = ((), (), s32[]{:S(2)}) async-start(), calls=%async_computation.1 | async-start | bytes 4734976 | tf_op jit(solution)/shard_map/all_gather | solution.py:336
  16.3 130.4 %all-gather.5.cloned.1.call-start = ((), (), s32[]{:S(2)}) async-start(), calls=%async_computation.2 | async-start | bytes 8912896 | tf_op jit(solution)/shard_map/all_gather | solution.py:337
  16.3 33.2 %copy-start.42 = (s32[8]{0:T(128)S(1)}, s32[8]{0:T(128)}, u32[]{:S(2)}) copy-start(s32[8]{0:T(128)} %param.18) | copy-start | bytes 100
  18.2 357.1 %reduce-scatter.2.cloned.1.call-start = ((), (), s32[]{:S(2)}) async-start(), calls=%async_computation.3 | async-start | bytes 8912896 | tf_op jit(solution)/shard_map/reduce_scatter | solution.py:278
  18.3 26.5 %collective-permute-start = (bf16[512,1024]{1,0:T(8,128)(2,1)}, bf16[512,1024]{1,0:T(8,128)(2,1)}, u32[]{:S(2)}, u32[]{:S(2)}) collective-permute-start(bf16[512,1024]{1,0:T(8,128)(2,1)} %param.16), channel_id=1, source_target_pairs={{0,1},{1,0},{2,3},{3,2},{4,5},{5,4},{6,7},{7,6},{8,9},{9,8},{10,11... | collective-permute-start | bytes 3145736 | tf_op jit(solution)/shard_map/ppermute | solution.py:223
  47.4 26.0 %copy-start.16 = (bf16[1024,1024]{1,0:T(8,128)(2,1)}, bf16[1024,1024]{1,0:T(8,128)(2,1)S(1)}, u32[]{:S(2)}) copy-start(bf16[1024,1024]{1,0:T(8,128)(2,1)S(1)} %maximum_select_fusion) | copy-start | bytes 6291460
  47.5 24.5 %collective-permute-start.1 = (bf16[512,1024]{1,0:T(8,128)(2,1)}, bf16[512,1024]{1,0:T(8,128)(2,1)S(1)}, u32[]{:S(2)}, u32[]{:S(2)}) collective-permute-start(bf16[512,1024]{1,0:T(8,128)(2,1)} %param.31), channel_id=1, source_target_pairs={{0,1},{1,0},{2,3},{3,2},{4,5},{5,4},{6,7},{7,6},{8,9},{9,8},{10,11... | collective-permute-start | bytes 3145736 | tf_op jit(solution)/shard_map/ppermute | solution.py:223
  49.7 152.7 %copy-start.38 = (pred[512]{0:T(512)(128)(4,1)}, pred[512]{0:T(512)(128)(4,1)S(1)}, u32[]{:S(2)}) copy-start(pred[512]{0:T(512)(128)(4,1)S(1)} %get-tuple-element.201) | copy-start | bytes 1540
  108.9 22.8 %collective-permute-start.2 = (bf16[512,1024]{1,0:T(8,128)(2,1)}, bf16[512,1024]{1,0:T(8,128)(2,1)}, u32[]{:S(2)}, u32[]{:S(2)}) collective-permute-start(bf16[512,1024]{1,0:T(8,128)(2,1)} %convolution_convert_fusion.3), channel_id=1, source_target_pairs={{0,1},{1,0},{2,3},{3,2},{4,5},{5,4},{6,7},{7,6},{8,9},{9,8},{10,11... | collective-permute-start | bytes 3145736 | tf_op jit(solution)/shard_map/ppermute | solution.py:223
  137.5 21.9 %collective-permute-start.3 = (bf16[512,1024]{1,0:T(8,128)(2,1)}, bf16[512,1024]{1,0:T(8,128)(2,1)}, u32[]{:S(2)}, u32[]{:S(2)}) collective-permute-start(bf16[512,1024]{1,0:T(8,128)(2,1)} %add_convert_fusion.2), channel_id=1, source_target_pairs={{0,1},{1,0},{2,3},{3,2},{4,5},{5,4},{6,7},{7,6},{8,9},{9,8},{10,11... | collective-permute-start | bytes 3145736 | tf_op jit(solution)/shard_map/ppermute | solution.py:223
  152.2 28.7 %copy-start.44 = (bf16[512,2048]{1,0:T(8,128)(2,1)}, bf16[512,2048]{1,0:T(8,128)(2,1)S(1)}, u32[]{:S(2)}) copy-start(bf16[512,2048]{1,0:T(8,128)(2,1)S(1)} %get-tuple-element.56) | copy-start | bytes 6291460
  164.0 16.8 %copy-start.46 = (bf16[512,2048]{1,0:T(8,128)(2,1)}, bf16[512,2048]{1,0:T(8,128)(2,1)S(1)}, u32[]{:S(2)}) copy-start(bf16[512,2048]{1,0:T(8,128)(2,1)S(1)} %get-tuple-element.57) | copy-start | bytes 6291460
  172.2 26.2 %collective-permute-start.4 = (bf16[512,1024]{1,0:T(8,128)(2,1)}, bf16[512,1024]{1,0:T(8,128)(2,1)}, u32[]{:S(2)}, u32[]{:S(2)}) collective-permute-start(bf16[512,1024]{1,0:T(8,128)(2,1)} %fusion.90), channel_id=1, source_target_pairs={{0,1},{1,0},{2,3},{3,2},{4,5},{5,4},{6,7},{7,6},{8,9},{9,8},{10,11... | collective-permute-start | bytes 3145736 | tf_op jit(solution)/shard_map/ppermute | solution.py:223
  208.0 23.9 %collective-permute-start.5 = (bf16[512,1024]{1,0:T(8,128)(2,1)}, bf16[512,1024]{1,0:T(8,128)(2,1)}, u32[]{:S(2)}, u32[]{:S(2)}) collective-permute-start(bf16[512,1024]{1,0:T(8,128)(2,1)} %convert_element_type.268), channel_id=1, source_target_pairs={{0,1},{1,0},{2,3},{3,2},{4,5},{5,4},{6,7},{7,6},{8,9},{9,8},{10,11... | collective-permute-start | bytes 3145736 | tf_op jit(solution)/shard_map/ppermute | solution.py:223
  237.0 7.3 %collective-permute-start.17 = (bf16[8,64,512]{2,1,0:T(8,128)(2,1)S(1)}, bf16[8,64,512]{2,1,0:T(8,128)(2,1)S(1)}, u32[]{:S(2)}, u32[]{:S(2)}) collective-permute-start(bf16[8,64,512]{2,1,0:T(8,128)(2,1)S(1)} %dynamic-slice_bitcast_fusion.2), channel_id=1, source_target_pairs={{0,2},{2,0},{4,6},{6,4},{8,10},{10,8},{12,14},{14,12},{16,18},{18,... | collective-permute-start | bytes 1572872 | tf_op jit(solution)/shard_map/ppermute | solution.py:292
  243.7 47.0 %collective-permute-start.6 = (bf16[512,1024]{1,0:T(8,128)(2,1)}, bf16[512,1024]{1,0:T(8,128)(2,1)}, u32[]{:S(2)}, u32[]{:S(2)}) collective-permute-start(bf16[512,1024]{1,0:T(8,128)(2,1)} %fusion.96), channel_id=1, source_target_pairs={{0,1},{1,0},{2,3},{3,2},{4,5},{5,4},{6,7},{7,6},{8,9},{9,8},{10,11... | collective-permute-start | bytes 3145736 | tf_op jit(solution)/shard_map/ppermute | solution.py:223
  244.5 8.5 %collective-permute-start.18 = (bf16[4,64,512]{2,1,0:T(8,128)(2,1)S(1)}, bf16[4,64,512]{2,1,0:T(8,128)(2,1)S(1)}, u32[]{:S(2)}, u32[]{:S(2)}) collective-permute-start(bf16[4,64,512]{2,1,0:T(8,128)(2,1)S(1)} %dynamic-slice_bitcast_fusion.4), channel_id=1, source_target_pairs={{0,4},{2,6},{4,0},{6,2},{8,12},{10,14},{12,8},{14,10},{16,20},{18,... | collective-permute-start | bytes 786440 | tf_op jit(solution)/shard_map/ppermute | solution.py:292
  253.1 10.3 %collective-permute-start.19 = (bf16[2,64,512]{2,1,0:T(8,128)(2,1)S(1)}, bf16[2,64,512]{2,1,0:T(8,128)(2,1)S(1)}, u32[]{:S(2)}, u32[]{:S(2)}) collective-permute-start(bf16[2,64,512]{2,1,0:T(8,128)(2,1)S(1)} %dynamic-slice_bitcast_fusion.5), channel_id=1, source_target_pairs={{0,8},{2,10},{4,12},{6,14},{8,0},{10,2},{12,4},{14,6},{16,24},{18,... | collective-permute-start | bytes 393224 | tf_op jit(solution)/shard_map/ppermute | solution.py:292
  264.1 24.9 %collective-permute-start.20 = (bf16[1,64,512]{2,1,0:T(8,128)(2,1)}, bf16[1,64,512]{2,1,0:T(8,128)(2,1)}, u32[]{:S(2)}, u32[]{:S(2)}) collective-permute-start(bf16[1,64,512]{2,1,0:T(8,128)(2,1)} %constant_dynamic-slice_fusion.2), channel_id=1, source_target_pairs={{0,16},{2,18},{4,20},{6,22},{8,24},{10,26},{12,28},{14,30},{16,0},... | collective-permute-start | bytes 196616 | tf_op jit(solution)/shard_map/ppermute | solution.py:292
  292.2 27.7 %slice-start = ((s8[4456448]{0:T(1024)(128)(4,1)}), s8[4194304]{0:T(1024)(128)(4,1)S(1)}, s32[]{:S(2)}) async-start(s8[4456448]{0:T(1024)(128)(4,1)} %bitcast.136), calls=%async_computation.4 | async-start | bytes 8388608
  296.1 23.8 %slice-start.1 = ((s8[4456448]{0:T(1024)(128)(4,1)}), s8[262144]{0:T(1024)(128)(4,1)S(1)}, s32[]{:S(2)}) async-start(s8[4456448]{0:T(1024)(128)(4,1)} %bitcast.136), calls=%async_computation.5 | async-start | bytes 524288
  296.1 23.8 %collective-permute-start.7 = (bf16[512,1024]{1,0:T(8,128)(2,1)S(1)}, bf16[512,1024]{1,0:T(8,128)(2,1)S(1)}, u32[]{:S(2)}, u32[]{:S(2)}) collective-permute-start(bf16[512,1024]{1,0:T(8,128)(2,1)S(1)} %fusion.82), channel_id=1, source_target_pairs={{0,1},{1,0},{2,3},{3,2},{4,5},{5,4},{6,7},{7,6},{8,9},{9,8},{10,11... | collective-permute-start | bytes 3145736 | tf_op jit(solution)/shard_map/ppermute | solution.py:223
  305.1 29.6 %collective-permute-start.13 = (bf16[8,64,1536]{2,1,0:T(8,128)(2,1)}, bf16[8,64,1536]{2,1,0:T(8,128)(2,1)S(1)}, u32[]{:S(2)}, u32[]{:S(2)}) collective-permute-start(bf16[8,64,1536]{2,1,0:T(8,128)(2,1)} %dynamic-slice_bitcast_fusion), channel_id=1, source_target_pairs={{0,2},{2,0},{4,6},{6,4},{8,10},{10,8},{12,14},{14,12},{16,18},{18,... | collective-permute-start | bytes 4718600 | tf_op jit(solution)/shard_map/ppermute | solution.py:292
  328.9 1.4 collective-permute-start.8
  330.4 4.3 %collective-permute-start.9 = (bf16[4,64,128]{2,1,0:T(8,128)(2,1)S(1)}, bf16[4,64,128]{2,1,0:T(8,128)(2,1)S(1)}, u32[]{:S(2)}, u32[]{:S(2)}) collective-permute-start(bf16[4,64,128]{2,1,0:T(8,128)(2,1)S(1)} %dynamic-slice_bitcast_fusion.7), channel_id=1, source_target_pairs={{0,4},{2,6},{4,0},{6,2},{8,12},{10,14},{12,8},{14,10},{16,20},{18,... | collective-permute-start | bytes 196616 | tf_op jit(solution)/shard_map/ppermute | solution.py:292
  336.9 18.5 %collective-permute-start.14 = (bf16[4,64,1536]{2,1,0:T(8,128)(2,1)S(1)}, bf16[4,64,1536]{2,1,0:T(8,128)(2,1)S(1)}, u32[]{:S(2)}, u32[]{:S(2)}) collective-permute-start(bf16[4,64,1536]{2,1,0:T(8,128)(2,1)S(1)} %dynamic-slice_bitcast_fusion.1), channel_id=1, source_target_pairs={{0,4},{2,6},{4,0},{6,2},{8,12},{10,14},{12,8},{14,10},{16,20},{18,... | collective-permute-start | bytes 2359304 | tf_op jit(solution)/shard_map/ppermute | solution.py:292
  337.2 3.9 %collective-permute-start.10 = (bf16[2,64,128]{2,1,0:T(8,128)(2,1)S(1)}, bf16[2,64,128]{2,1,0:T(8,128)(2,1)S(1)}, u32[]{:S(2)}, u32[]{:S(2)}) collective-permute-start(bf16[2,64,128]{2,1,0:T(8,128)(2,1)S(1)} %dynamic-slice_bitcast_fusion.8), channel_id=1, source_target_pairs={{0,8},{2,10},{4,12},{6,14},{8,0},{10,2},{12,4},{14,6},{16,24},{18,... | collective-permute-start | bytes 98312 | tf_op jit(solution)/shard_map/ppermute | solution.py:292
  341.1 14.7 %collective-permute-start.11 = (bf16[1,64,128]{2,1,0:T(8,128)(2,1)S(1)}, bf16[1,64,128]{2,1,0:T(8,128)(2,1)S(1)}, u32[]{:S(2)}, u32[]{:S(2)}) collective-permute-start(bf16[1,64,128]{2,1,0:T(8,128)(2,1)S(1)} %constant_dynamic-slice_fusion.1), channel_id=1, source_target_pairs={{0,16},{2,18},{4,20},{6,22},{8,24},{10,26},{12,28},{14,30},{16,0},... | collective-permute-start | bytes 49160 | tf_op jit(solution)/shard_map/ppermute | solution.py:292
  355.7 9.2 %collective-permute-start.15 = (bf16[2,64,1536]{2,1,0:T(8,128)(2,1)S(1)}, bf16[2,64,1536]{2,1,0:T(8,128)(2,1)S(1)}, u32[]{:S(2)}, u32[]{:S(2)}) collective-permute-start(bf16[2,64,1536]{2,1,0:T(8,128)(2,1)S(1)} %dynamic-slice_bitcast_fusion.3), channel_id=1, source_target_pairs={{0,8},{2,10},{4,12},{6,14},{8,0},{10,2},{12,4},{14,6},{16,24},{18,... | collective-permute-start | bytes 1179656 | tf_op jit(solution)/shard_map/ppermute | solution.py:292
  355.9 12.9 %collective-permute-start.12 = (f32[6,64]{0,1:T(8,128)S(1)}, f32[6,64]{0,1:T(8,128)S(1)}, u32[]{:S(2)}, u32[]{:S(2)}) collective-permute-start(f32[6,64]{0,1:T(8,128)S(1)} %slice_bitcast_fusion.1), channel_id=1, source_target_pairs={{0,1},{1,0},{2,3},{3,2},{4,5},{5,4},{6,7},{7,6},{8,9},{9,8},{10,11... | collective-permute-start | bytes 4616 | tf_op jit(solution)/shard_map/ppermute | solution.py:223
  365.0 9.1 %collective-permute-start.16 = (bf16[1,64,1536]{2,1,0:T(8,128)(2,1)S(1)}, bf16[1,64,1536]{2,1,0:T(8,128)(2,1)S(1)}, u32[]{:S(2)}, u32[]{:S(2)}) collective-permute-start(bf16[1,64,1536]{2,1,0:T(8,128)(2,1)S(1)} %constant_dynamic-slice_fusion), channel_id=1, source_target_pairs={{0,16},{2,18},{4,20},{6,22},{8,24},{10,26},{12,28},{14,30},{16,0},... | collective-permute-start | bytes 589832 | tf_op jit(solution)/shard_map/ppermute | solution.py:292
  (44 other events, 245.3 us)
Sparse Core Ops, SparseCore 0:
  16.4 54.6 all-gather.2
  73.3 73.4 all-gather.4
  222.3 108.0 reduce-scatter.1
